TPU v7x, 128 devices: a whole 4x4x4 slice. The times are simulated.
128 devices in a mesh: group: 4 (over y), tp: 32 (over z, x, core).
Axes of the slice: x: 4, y: 4, z: 4, core: 2. Of those that a mesh axis runs over, the one named last changes fastest.
Arguments:
- tokens: bfloat16 [8192, 8192], P(('group', 'tp')), may hold values from -6 to 6
- query_weight_matrix: bfloat16 [8192, 8192], P(None, 'tp'), may hold values from -0.0625 to 0.0625
- adapter_down_weight: bfloat16 [512, 64, 8192], P('group', 'tp'), may hold values from -0.0625 to 0.0625
- adapter_up_weight: bfloat16 [512, 64, 8192], P('group', None, 'tp'), may hold values from -0.75 to 0.75
- lengths: int32 [4, 16], replicated, may hold values from 1 to 1024, 2048 in all within a row
- request_adapter_id: int32 [4, 16], replicated, may hold values from 0 to 511, as said below
- adapter_storage_slot: int32 [512], replicated, may hold values from 0 to 511, as said below
Outputs:
- query: bfloat16 [8192, 8192], P('group', 'tp')
Inputs may be any that keep to these rules, and one draw needn't show every extreme that they name: `request_adapter_id`: no more than 6 requests of one group use adapters whose slots lie on one owner group (slot s lies on owner group s // 128); every group reaches 6 on some owner group. `adapter_storage_slot`: A permutation of the slots.
All inputs are finite; a program needn't handle non-finite values.
Results may differ from a plain program's by a relative error of at most 0.003.
Values may be sent and summed in bfloat16 or wider, within the bound.
A program may use at most 192 MiB of HBM per device.

v0:
```python
import jax
import jax.numpy as jnp
from jax import lax
from jax.sharding import PartitionSpec as P

CAP = 6


adapter_scale = 0.5


def fetch_pieces(down_token_rows, up_token_rows):
    return (
        lax.all_to_all(down_token_rows, "group", split_axis=0, concat_axis=0, tiled=True),
        lax.all_to_all(up_token_rows, "group", split_axis=0, concat_axis=0, tiled=True),
    )


def local(
    tokens,
    query_weight_matrix,
    adapter_down_weight,
    adapter_up_weight,
    lengths,
    request_adapter_id,
    adapter_storage_slot,
):
    groups = lax.axis_size("group")
    my_group = lax.axis_index("group")
    local_adapter_count = adapter_down_weight.shape[0]
    low_rank_hidden = adapter_down_weight.shape[1]
    width = tokens.shape[1]
    columns = query_weight_matrix.shape[1]
    full_rank_output = adapter_up_weight.shape[1]
    requests = lengths.shape[1]
    request_slots = groups * CAP
    group_rows = tokens.shape[0] * lax.axis_size("tp")
    adapter_ids = jnp.arange(adapter_storage_slot.shape[0], dtype=jnp.int32)
    slot_of = jnp.sum(
        jnp.where(
            request_adapter_id[:, :, None] == adapter_ids[None, None, :],
            adapter_storage_slot[None, None, :],
            0,
        ),
        axis=2,
    )
    owner = slot_of // local_adapter_count
    local_index = slot_of % local_adapter_count
    order = jnp.arange(requests, dtype=jnp.int32)
    same_owner = owner[:, :, None] == owner[:, None, :]
    earlier = order[None, :] < order[:, None]
    rank_in = jnp.sum((same_owner & earlier[None]).astype(jnp.int32), axis=2)
    places = jnp.arange(CAP, dtype=jnp.int32)
    chosen = (owner[:, None, :] == my_group) & (rank_in[:, None, :] == places[None, :, None])
    adapter_indices = jnp.sum(jnp.where(chosen, local_index[:, None, :], 0), axis=2).reshape(-1)
    present_adapters = jnp.any(chosen, axis=2).reshape(-1)
    down_token_rows = jnp.where(
        present_adapters[:, None, None],
        adapter_down_weight[adapter_indices],
        jnp.zeros((), adapter_down_weight.dtype),
    )
    up_token_rows = jnp.where(
        present_adapters[:, None, None],
        adapter_up_weight[adapter_indices],
        jnp.zeros((), adapter_up_weight.dtype),
    )
    down_token_rows = down_token_rows.reshape(groups, CAP, low_rank_hidden, width)
    up_token_rows = up_token_rows.reshape(groups, CAP, full_rank_output, columns)
    my_lengths = lax.dynamic_index_in_dim(lengths, my_group, 0, keepdims=False)
    my_owner = lax.dynamic_index_in_dim(owner, my_group, 0, keepdims=False)
    my_rank = lax.dynamic_index_in_dim(rank_in, my_group, 0, keepdims=False)
    ends = jnp.cumsum(my_lengths)
    position = jnp.arange(group_rows, dtype=jnp.int32)
    request_of = jnp.sum((position[:, None] >= ends[None, :]).astype(jnp.int32), axis=1)
    slot_index = my_owner * CAP + my_rank
    token_slot = jnp.sum(
        jnp.where(request_of[:, None] == order[None, :], slot_index[None, :], 0), axis=1
    )
    selector = (token_slot[:, None] == jnp.arange(request_slots, dtype=jnp.int32)[None, :]).astype(
        jnp.float32
    )
    contract = (((1,), (1,)), ((), ()))
    gathered = lax.all_gather(tokens, "tp", axis=0, tiled=True)
    base_output = jnp.dot(gathered, query_weight_matrix, preferred_element_type=jnp.float32)
    a_recv, b_recv = fetch_pieces(down_token_rows, up_token_rows)
    a_flat = a_recv.reshape(request_slots * low_rank_hidden, width)
    partial_value = lax.dot_general(gathered, a_flat, contract, preferred_element_type=jnp.float32)
    shrink_float = jnp.sum(
        partial_value.reshape(group_rows, request_slots, low_rank_hidden) * selector[:, :, None],
        axis=1,
    )
    shrink_part = shrink_float.astype(jnp.bfloat16)
    shrink = lax.all_gather(shrink_part, "tp", axis=1, tiled=True)
    b_table = b_recv.reshape(request_slots, full_rank_output, columns)
    block_rows = min(512, group_rows)
    block_count = group_rows // block_rows

    def up_block(inputs):
        codes_block, slots_block = inputs
        b_tokens = b_table[slots_block]
        return jnp.einsum("tr,trc->tc", codes_block, b_tokens, preferred_element_type=jnp.float32)

    adapter_update = lax.map(
        up_block,
        (
            shrink.reshape(block_count, block_rows, full_rank_output),
            token_slot.reshape(block_count, block_rows),
        ),
    )
    adapter_update = adapter_update.reshape(group_rows, columns)
    return (base_output + adapter_scale * adapter_update).astype(jnp.bfloat16)


def solution(mesh):
    placed = (
        P(("group", "tp"), None),
        P(None, "tp"),
        P("group", "tp", None),
        P("group", None, "tp"),
        P(),
        P(),
        P(),
    )
    return jax.shard_map(
        local, mesh=mesh, in_specs=placed, out_specs=P("group", "tp"), check_vma=False
    )
```

profile of v0, /device:TPU:1, one launch (start us, length us, event | category | flops | bytes accessed | tf_op | source)
XLA Modules:
  0.0 282.3 jit_solution(17939618233316259864)
XLA Ops:
  6.5 0.0 copy-start
  6.5 0.0 all-gather.3.cloned.1.call-start
  6.5 0.7 all-gather.3.cloned.1.call-update
  7.3 0.9 select_reduce_fusion.1
  8.2 0.2 convert_reduce_fusion.1
  8.4 0.2 select_reduce_fusion.2
  8.6 0.1 copy.14
  8.7 0.1 reshape.199
  8.8 0.2 fusion.5
  9.0 0.1 copy.13
  9.1 4.3 %gather_fusion.1 = bf16[24,2,8192]{2,1,0:T(2,128)(2,1)S(1)} fusion(bf16[128,2,8192]{2,1,0:T(2,128)(2,1)} %param.11, s32[1024]{0:T(1024)S(1)} %pad_clamp_fusion.1), kind=kCustom, calls=%fused_computation.1 | custom fusion | bytes 1572960 | tf_op jit(solution)/shard_map/gather | solution.py:59
  13.5 1.6 broadcast_select_fusion
  15.1 5.0 %all-to-all-start = ((bf16[4,6,2,8192]{3,2,1,0:T(2,128)(2,1)}), bf16[4,6,2,8192]{3,2,1,0:T(2,128)(2,1)S(1)}, u32[]{:S(2)}, u32[]{:S(2)}) async-start(bf16[4,6,2,8192]{3,2,1,0:T(2,128)(2,1)} %broadcast_select_fusion), calls=%async_computation | async-start | bytes 1572864 | tf_op jit(solution)/shard_map/all_to_all | solution.py:14
  20.1 0.0 copy-done
  20.1 0.1 copy.15
  20.2 0.1 reduce
  20.4 0.1 convert_reduce_fusion
  20.5 0.1 select_reduce_fusion
  20.6 3.0 %gather_fusion.2 = bf16[24,64,256]{2,1,0:T(8,128)(2,1)S(1)} fusion(bf16[128,64,256]{2,1,0:T(8,128)(2,1)} %param.12, s32[1024]{0:T(1024)S(1)} %pad_clamp_fusion.1), kind=kCustom, calls=%fused_computation.2 | custom fusion | bytes 1572960 | tf_op jit(solution)/shard_map/gather | solution.py:64
  23.5 1.0 broadcast_select_fusion.1
  24.6 6.9 %all-to-all-done = bf16[4,6,2,8192]{3,2,1,0:T(2,128)(2,1)S(1)} async-done(((bf16[4,6,2,8192]{3,2,1,0:T(2,128)(2,1)}), bf16[4,6,2,8192]{3,2,1,0:T(2,128)(2,1)S(1)}, u32[]{:S(2)}, u32[]{:S(2)}) %all-to-all-start) | async-done | bytes 786464 | tf_op jit(solution)/shard_map/all_to_all | solution.py:14
  31.5 3.5 %all-to-all-start.1 = ((bf16[4,6,64,256]{3,2,1,0:T(8,128)(2,1)}), bf16[4,6,64,256]{3,2,1,0:T(8,128)(2,1)S(1)}, u32[]{:S(2)}, u32[]{:S(2)}) async-start(bf16[4,6,64,256]{3,2,1,0:T(8,128)(2,1)} %broadcast_select_fusion.1), calls=%async_computation.1 | async-start | bytes 1572864 | tf_op jit(solution)/shard_map/all_to_all | solution.py:15
  35.0 0.3 reshape.200
  35.3 92.0 %all-gather.3.cloned.1.call-done = bf16[2048,8192]{1,0:T(8,128)(2,1)} async-done(((bf16[64,8192]{1,0:T(8,128)(2,1)}), bf16[2048,8192]{1,0:T(8,128)(2,1)}) %all-gather.3.cloned.1.call-update) | async-done | bytes 33554448 | tf_op jit(solution)/shard_map/all_gather | solution.py:83
  127.3 15.2 %convolution_bitcast_fusion = f32[2048,48]{0,1:T(8,128)S(1)} fusion(bf16[48,8192]{1,0:T(8,128)(2,1)S(1)} %reshape.200, bf16[2048,8192]{1,0:T(8,128)(2,1)} %all-gather.3.cloned.1.call-done), kind=kOutput, calls=%fused_computation.11 | convolution fusion | flops 1610612736 | bytes 34734080 | tf_op jit(solution)/shard_map/dot_general | solution.py:87
  142.5 0.2 reshape.201
  142.8 0.2 multiply_reduce_fusion
  143.0 24.6 %all-gather = bf16[32,2,2048]{2,1,0:T(2,128)(2,1)S(1)} all-gather(bf16[1,2,2048]{2,1,0:T(2,128)(2,1)S(1)} %bitcast.52), channel_id=1, replica_groups=mesh['group'=4,'tp'=32] {'tp'}, dimensions={0}, use_global_device_ids=true | all-gather | bytes 270336 | tf_op jit(solution)/shard_map/all_gather | solution.py:93
  167.6 0.1 reshape.232
  167.7 0.3 copy.20
  168.0 0.0 all-to-all-done.1
  168.0 88.2 %while.10 = (s32[]{:T(128)}, f32[4,512,256]{2,1,0:T(8,128)}, bf16[4,512,64]{2,1,0:T(8,128)(2,1)S(1)}, s32[4,512]{1,0:T(4,128)S(1)}, bf16[24,64,256]{2,1,0:T(8,128)(2,1)S(1)}, /*index=5*/s32[]{:T(128)}) while((s32[]{:T(128)}, f32[4,512,256]{2,1,0:T(8,128)}, bf16[4,512,64]{2,1,0:T(8,128)(2,1)S(1)}, s32[4,512]{1,0:T(4,128)S(1)}, ...), condition=%wide.region_9.10_spmd, body=%wide.region_8.9_spmd.sunk | while | flops 16779776 | bytes 52113996 | solution.py:103
  168.1 13.7 %gather_fusion = bf16[512,64,256]{2,1,0:T(8,128)(2,1)} fusion(bf16[24,64,256]{2,1,0:T(8,128)(2,1)S(1)} %get-tuple-element.107, s32[1024]{0:T(1024)S(1)} %pad_clamp_fusion.3), kind=kCustom, calls=%fused_computation.clone.1 | custom fusion | bytes 33556480 | tf_op jit(solution)/shard_map/while/body/eval_jaxpr/gather | solution.py:100
  181.8 8.1 %fusion.22 = f32[512,1,256]{2,1,0:T(1,128)S(1)} fusion(bf16[512,64,256]{2,1,0:T(8,128)(2,1)} %gather_fusion, bf16[512,64,1]{1,0,2:T(8,128)(2,1)S(1)} %dynamic-slice_bitcast_fusion.2), kind=kOutput, calls=%fused_computation.4.clone.1 | convolution fusion | flops 16777216 | bytes 17367040 | tf_op jit(solution)/shard_map/while/body/eval_jaxpr/tr,trc->tc/dot_general | solution.py:101
  189.8 0.8 bitcast_dynamic-update-slice_fusion.2
  190.7 12.6 %gather_fusion = bf16[512,64,256]{2,1,0:T(8,128)(2,1)} fusion(bf16[24,64,256]{2,1,0:T(8,128)(2,1)S(1)} %get-tuple-element.107, s32[1024]{0:T(1024)S(1)} %pad_clamp_fusion.3), kind=kCustom, calls=%fused_computation.clone.1 | custom fusion | bytes 33556480 | tf_op jit(solution)/shard_map/while/body/eval_jaxpr/gather | solution.py:100
  203.4 8.1 %fusion.22 = f32[512,1,256]{2,1,0:T(1,128)S(1)} fusion(bf16[512,64,256]{2,1,0:T(8,128)(2,1)} %gather_fusion, bf16[512,64,1]{1,0,2:T(8,128)(2,1)S(1)} %dynamic-slice_bitcast_fusion.2), kind=kOutput, calls=%fused_computation.4.clone.1 | convolution fusion | flops 16777216 | bytes 17367040 | tf_op jit(solution)/shard_map/while/body/eval_jaxpr/tr,trc->tc/dot_general | solution.py:101
  211.4 0.8 bitcast_dynamic-update-slice_fusion.2
  212.3 12.8 %gather_fusion = bf16[512,64,256]{2,1,0:T(8,128)(2,1)} fusion(bf16[24,64,256]{2,1,0:T(8,128)(2,1)S(1)} %get-tuple-element.107, s32[1024]{0:T(1024)S(1)} %pad_clamp_fusion.3), kind=kCustom, calls=%fused_computation.clone.1 | custom fusion | bytes 33556480 | tf_op jit(solution)/shard_map/while/body/eval_jaxpr/gather | solution.py:100
  225.1 8.1 %fusion.22 = f32[512,1,256]{2,1,0:T(1,128)S(1)} fusion(bf16[512,64,256]{2,1,0:T(8,128)(2,1)} %gather_fusion, bf16[512,64,1]{1,0,2:T(8,128)(2,1)S(1)} %dynamic-slice_bitcast_fusion.2), kind=kOutput, calls=%fused_computation.4.clone.1 | convolution fusion | flops 16777216 | bytes 17367040 | tf_op jit(solution)/shard_map/while/body/eval_jaxpr/tr,trc->tc/dot_general | solution.py:101
  233.2 0.8 bitcast_dynamic-update-slice_fusion.2
  234.1 13.2 %gather_fusion = bf16[512,64,256]{2,1,0:T(8,128)(2,1)} fusion(bf16[24,64,256]{2,1,0:T(8,128)(2,1)S(1)} %get-tuple-element.107, s32[1024]{0:T(1024)S(1)} %pad_clamp_fusion.3), kind=kCustom, calls=%fused_computation.clone.1 | custom fusion | bytes 33556480 | tf_op jit(solution)/shard_map/while/body/eval_jaxpr/gather | solution.py:100
  247.3 8.1 %fusion.22 = f32[512,1,256]{2,1,0:T(1,128)S(1)} fusion(bf16[512,64,256]{2,1,0:T(8,128)(2,1)} %gather_fusion, bf16[512,64,1]{1,0,2:T(8,128)(2,1)S(1)} %dynamic-slice_bitcast_fusion.2), kind=kOutput, calls=%fused_computation.4.clone.1 | convolution fusion | flops 16777216 | bytes 17367040 | tf_op jit(solution)/shard_map/while/body/eval_jaxpr/tr,trc->tc/dot_general | solution.py:101
  255.4 0.8 bitcast_dynamic-update-slice_fusion.2
  256.2 0.0 copy-start.2
  256.2 1.9 broadcast_multiply_fusion
  258.1 0.9 copy-done.2
  259.0 0.0 copy-start.1
  259.0 16.4 %fusion.2 = bf16[2048,256]{1,0:T(8,128)(2,1)} fusion(f32[2048,256]{1,0:T(8,128)S(1)} %bitcast.49, bf16[2048,8192]{1,0:T(8,128)(2,1)} %all-gather.3.cloned.1.call-done, bf16[8192,256]{1,0:T(8,128)(2,1)S(1)} %copy-done.2), kind=kOutput, calls=%fused_computation.10 | convolution fusion | flops 8590983168 | bytes 40894464 | tf_op jit(solution)/shard_map/dot_general | solution.py:84
  275.4 0.0 copy-done.1
  (23 shorter events, 0.2 us)
Async XLA Ops:
  6.5 13.6 %copy-start = (s32[4,16]{1,0:T(4,128)S(1)}, s32[4,16]{1,0:T(4,128)}, u32[]{:S(2)}) copy-start(s32[4,16]{1,0:T(4,128)} %param.13) | copy-start | bytes 772
  6.5 120.8 %all-gather.3.cloned.1.call-start = ((), (), s32[]{:S(2)}) async-start(), calls=%async_computation.2 | async-start | bytes 34603008 | tf_op jit(solution)/shard_map/all_gather | solution.py:83
  15.1 16.4 %all-to-all-start = ((bf16[4,6,2,8192]{3,2,1,0:T(2,128)(2,1)}), bf16[4,6,2,8192]{3,2,1,0:T(2,128)(2,1)S(1)}, u32[]{:S(2)}, u32[]{:S(2)}) async-start(bf16[4,6,2,8192]{3,2,1,0:T(2,128)(2,1)} %broadcast_select_fusion), calls=%async_computation | async-start | bytes 1572864 | tf_op jit(solution)/shard_map/all_to_all | solution.py:14
  31.5 136.5 %all-to-all-start.1 = ((bf16[4,6,64,256]{3,2,1,0:T(8,128)(2,1)}), bf16[4,6,64,256]{3,2,1,0:T(8,128)(2,1)S(1)}, u32[]{:S(2)}, u32[]{:S(2)}) async-start(bf16[4,6,64,256]{3,2,1,0:T(8,128)(2,1)} %broadcast_select_fusion.1), calls=%async_computation.1 | async-start | bytes 1572864 | tf_op jit(solution)/shard_map/all_to_all | solution.py:15
  256.2 2.8 copy-start.2
  259.0 16.4 %copy-start.1 = (s32[4,16]{1,0:T(4,128)S(1)}, s32[4,16]{1,0:T(4,128)}, u32[]{:S(2)}) copy-start(s32[4,16]{1,0:T(4,128)} %param.13) | copy-start | bytes 772
Sparse Core Ops, SparseCore 0:
  9.6 117.6 all-gather.2
where the time goes:
time: 283 us; the launch traced here: 282 us
  waiting for transfers between devices  99.6 us (35%)
  local copies, waits for them, and re-layouts  65.3 us (23%)
  matrix products  63.9 us (23%)
  blocking collectives  24.6 us (9%)
  between operations  13.5 us (5%)
  starting transfers between devices  8.51 us (3%)
  other arithmetic  6.72 us (2%)
    all_gather x1, waiting for transfers between devices, local(): gathered = lax.all_gather(tokens, 'tp', axis=0, tiled=True)  92 us
    gather x4, local copies, waits for them, and re-layouts, up_block(): b_tokens = b_table[slots_block]  52.4 us
    dot_general x4, matrix products, up_block(): jnp.einsum('tr,trc->tc', codes_block, b_tokens, preferred_element_type=jn...  32.3 us
    all_gather x1, blocking collectives, local(): shrink = lax.all_gather(shrink_part, 'tp', axis=1, tiled=True)  24.6 us
    dot_general x1, matrix products, local(): jnp.dot(gathered, query_weight_matrix, preferred_element_type=jnp.float32)  16.4 us
    dot_general x1, matrix products, local(): lax.dot_general(gathered, a_flat, contract, preferred_element_type=jnp.fl...  15.2 us
    all_to_all x1, waiting for transfers between devices, fetch_pieces(): lax.all_to_all(down_token_rows, 'group', split_axis=0, concat_axis=0, til...  6.88 us
  transfers between devices with their start and end apart: 3, of which 2 were waited for; matrix products, arithmetic and copies ran while one was open for 10% of the time, Pallas kernels for 0%

commit v1 on v0

v1 whole, which is shorter than its diff:
```python
import jax
import jax.numpy as jnp
from jax import lax
from jax.experimental import pallas as pl
from jax.experimental.pallas import tpu as pltpu
from jax.sharding import PartitionSpec as P

MESH = pl.DeviceIdType.MESH
F32 = jnp.float32
BF16 = jnp.bfloat16

CAP = 6
GROUPS = 4
REQUESTS = 16
RANK = 64
WIDTH = 8192
COLS = 256
SHARD = 64
HALVES = 2
HALF = SHARD // HALVES
SOURCES = 8
HROWS = SOURCES * HALF
NK = 4
KC = WIDTH // NK
WC = KC // 4
PIECES = HALVES * NK
OWNED = 128

LEFT, RIGHT, FAR, ACROSS, ACROSS_LEFT, ACROSS_RIGHT, ACROSS_FAR = range(7)


def kernel(
    tok_hbm, w_hbm, down_hbm, up_hbm, len_ref, rid_ref, slot_ref, out_hbm,
    tok, wbuf, dloc, uloc, dsend, usend, drecv, urecv, dtmp, dc, uc, acc, part, shr, ost,
    loc_sem, own_sem, tok_ss, tok_rs, w_ss, w_rs, ws_ss, ws_rs, wf_ss, wf_rs,
    ad_ss, ad_rs, cp_ss, cp_rs, sh_ss, sh_rs, out_ss, out_rs,
):
    g = lax.axis_index("group")
    tp = lax.axis_index("tp")
    z = tp // 8
    x = (tp // 2) % 4
    c = tp % 2
    side = z // 2
    bit = z % 2
    z_across = 2 * side + 1 - bit
    z_partner = 3 - z

    def device(zz, xx, cc, gg=None):
        return (g if gg is None else gg, (zz * 4 + xx) * 2 + cc)

    left, right, far = (x + 3) % 4, (x + 1) % 4, (x + 2) % 4
    to_left, to_right = device(z, left, c), device(z, right, c)
    to_across = device(z_across, x, c)
    to_sibling = device(z, x, 1 - c)
    to_partner = device(z_partner, x, c)
    to_partner_other = device(z_partner, x, 1 - c)

    sends = []

    def send(src, dst, ss, rs, dev):
        copy = pltpu.make_async_remote_copy(
            src_ref=src, dst_ref=dst, send_sem=ss, recv_sem=rs, device_id=dev, device_id_type=MESH
        )
        copy.start()
        sends.append(copy)

    def arrived(dst, rs):
        pltpu.make_async_copy(dst, dst, rs).wait()

    down_copy = pltpu.make_async_copy(down_hbm, dloc, loc_sem.at[0])
    up_copy = pltpu.make_async_copy(up_hbm, uloc, loc_sem.at[1])
    mine = bit * 4 + x
    tok_copy = pltpu.make_async_copy(tok_hbm, tok.at[mine], loc_sem.at[2])
    w_copies = [
        pltpu.make_async_copy(
            w_hbm.at[pl.ds(i * KC, KC)], wbuf.at[0, pl.ds(i * KC, KC)], own_sem.at[i]
        )
        for i in range(NK)
    ]
    down_copy.start()
    up_copy.start()
    tok_copy.start()
    for copy in w_copies:
        copy.start()

    peers = [device(z, xx, c) for xx in (left, right, far)]
    peers += [device(z_across, xx, c) for xx in (x, left, right, far)]
    near = list(peers)
    peers += [to_sibling, to_partner, to_partner_other]
    peers += [device(z, x, c, (g + d) % GROUPS) for d in (1, 2, 3)]
    barrier = pltpu.get_barrier_semaphore()
    for dev in peers:
        pl.semaphore_signal(barrier, inc=1, device_id=dev, device_id_type=MESH)
    pl.semaphore_wait(barrier, len(peers))

    def at(source, p):
        r, k = divmod(p, NK)
        return tok.at[source, pl.ds(r * HALF, HALF), pl.ds(k * KC, KC)]

    def tok_send(source, p, n, cls, dev):
        send(at(source, p), at(source, p), tok_ss.at[n, p], tok_rs.at[cls, p], dev)

    s_left, s_right, s_far = bit * 4 + left, bit * 4 + right, bit * 4 + far
    other = (1 - bit) * 4
    a_mine, a_left, a_right, a_far = other + x, other + left, other + right, other + far

    def across_first(p):
        return p % 2 == 0

    def relay_right(p):
        return (p // 2) % 2 == 0

    def own_send(p):
        r, k = divmod(p, NK)
        src = tok_hbm.at[pl.ds(r * HALF, HALF), pl.ds(k * KC, KC)]
        send(src, at(mine, p), tok_ss.at[0, p], tok_rs.at[ACROSS, p], to_across)
        send(src, at(mine, p), tok_ss.at[1, p], tok_rs.at[LEFT, p], to_right)
        send(src, at(mine, p), tok_ss.at[2, p], tok_rs.at[RIGHT, p], to_left)

    def tok_first(p):
        arrived(at(a_mine, p), tok_rs.at[ACROSS, p])
        if across_first(p):
            tok_send(a_mine, p, 3, ACROSS_LEFT, to_right)
            tok_send(a_mine, p, 4, ACROSS_RIGHT, to_left)
        arrived(at(s_left, p), tok_rs.at[LEFT, p])
        if relay_right(p):
            tok_send(s_left, p, 5, FAR, to_right)
        if not across_first(p):
            tok_send(s_left, p, 3, ACROSS_LEFT, to_across)
        arrived(at(s_right, p), tok_rs.at[RIGHT, p])
        if not relay_right(p):
            tok_send(s_right, p, 5, FAR, to_left)
        if not across_first(p):
            tok_send(s_right, p, 4, ACROSS_RIGHT, to_across)

    def tok_second(p):
        if across_first(p):
            arrived(at(a_left, p), tok_rs.at[ACROSS_LEFT, p])
            if relay_right(p):
                tok_send(a_left, p, 6, ACROSS_FAR, to_right)
            arrived(at(a_right, p), tok_rs.at[ACROSS_RIGHT, p])
            if not relay_right(p):
                tok_send(a_right, p, 6, ACROSS_FAR, to_left)
            arrived(at(s_far, p), tok_rs.at[FAR, p])
        else:
            arrived(at(s_far, p), tok_rs.at[FAR, p])
            tok_send(s_far, p, 6, ACROSS_FAR, to_across)
            arrived(at(a_left, p), tok_rs.at[ACROSS_LEFT, p])
            arrived(at(a_right, p), tok_rs.at[ACROSS_RIGHT, p])

    def tok_third(p):
        arrived(at(a_far, p), tok_rs.at[ACROSS_FAR, p])

    def w_rows(i, q):
        return pl.ds(i * KC + q * WC, WC)

    def w_own_send(i):
        rows = w_rows(i, g)
        send(w_hbm.at[rows], wbuf.at[2, rows], w_ss.at[0, i], w_rs.at[0, i], to_partner)

    def w_sibling_send(i):
        rows = pl.ds(i * KC, KC)
        send(w_hbm.at[rows], wbuf.at[1, rows], ws_ss.at[i], ws_rs.at[i], to_sibling)

    g_next, g_prev, g_far = (g + 1) % GROUPS, (g + 3) % GROUPS, (g + 2) % GROUPS
    to_next, to_prev = device(z, x, c, g_next), device(z, x, c, g_prev)

    def w_forward(i, q, cls):
        rows = w_rows(i, q)
        send(wbuf.at[2, rows], wbuf.at[3, rows], wf_ss.at[cls, i], wf_rs.at[cls, i], to_sibling)

    def w_send(i, q, n, cls, dev):
        rows = w_rows(i, q)
        send(wbuf.at[2, rows], wbuf.at[2, rows], w_ss.at[n, i], w_rs.at[cls, i], dev)

    def w_first(i):
        arrived(wbuf.at[2, w_rows(i, g)], w_rs.at[0, i])
        w_send(i, g, 1, 1, to_next)
        w_send(i, g, 2, 3, to_prev)
        w_forward(i, g, 0)

    def w_second(i):
        arrived(wbuf.at[2, w_rows(i, g_prev)], w_rs.at[1, i])
        if i % 2 == 0:
            w_send(i, g_prev, 3, 2, to_next)
        w_forward(i, g_prev, 1)
        arrived(wbuf.at[2, w_rows(i, g_next)], w_rs.at[3, i])
        if i % 2 == 1:
            w_send(i, g_next, 3, 2, to_prev)
        w_forward(i, g_next, 3)

    def w_third(i):
        arrived(wbuf.at[2, w_rows(i, g_far)], w_rs.at[2, i])
        w_forward(i, g_far, 2)

    def w_ready(i):
        w_copies[i].wait()
        arrived(wbuf.at[1, pl.ds(i * KC, KC)], ws_rs.at[i])
        for cls, q in enumerate((g, g_prev, g_far, g_next)):
            arrived(wbuf.at[3, w_rows(i, q)], wf_rs.at[cls, i])

    def adapters_pick():
        picked = []
        for dest in range(GROUPS):
            index = [jnp.int32(0)] * CAP
            count = jnp.int32(0)
            for j in range(REQUESTS):
                slot = slot_ref[rid_ref[dest, j]]
                is_mine = slot // OWNED == g
                local = slot % OWNED
                for p in range(min(CAP, j + 1)):
                    index[p] = jnp.where(is_mine & (count == p), local, index[p])
                count = count + is_mine.astype(jnp.int32)
            picked.append(index)
        down_copy.wait()
        for dest in range(GROUPS):
            for p in range(CAP):
                dsend[dest * CAP + p] = dloc[picked[dest][p]]
        for d in (1, 3, 2):
            rows = pl.ds(((g + d) % GROUPS) * CAP, CAP)
            dev = device(z, x, c, (g + d) % GROUPS)
            send(dsend.at[rows], drecv.at[pl.ds(g * CAP, CAP)], ad_ss.at[0, d], ad_rs.at[0, d], dev)
        up_copy.wait()
        for dest in range(GROUPS):
            for p in range(CAP):
                usend[dest * CAP + p] = uloc[picked[dest][p]]
        for d in (1, 3, 2):
            rows = pl.ds(((g + d) % GROUPS) * CAP, CAP)
            dev = device(z, x, c, (g + d) % GROUPS)
            send(usend.at[rows], urecv.at[pl.ds(g * CAP, CAP)], ad_ss.at[1, d], ad_rs.at[1, d], dev)
        rows = pl.ds(g * CAP, CAP)
        for n, (src, dst) in enumerate(((dsend, drecv), (usend, urecv))):
            pltpu.make_async_copy(src.at[rows], dst.at[rows], ad_ss.at[n, 0]).start()

    def request_places():
        places = []
        counts = [jnp.int32(0)] * GROUPS
        for j in range(REQUESTS):
            owner = slot_ref[rid_ref[g, j]] // OWNED
            place = jnp.int32(0)
            for o in range(GROUPS):
                hit = owner == o
                place = place + jnp.where(hit, o * CAP + counts[o], 0)
                counts[o] = counts[o] + hit.astype(jnp.int32)
            places.append(place)
        return places

    def adapters_arrived(n, ref, src):
        rows = pl.ds(g * CAP, CAP)
        pltpu.make_async_copy(src.at[rows], ref.at[rows], ad_ss.at[n, 0]).wait()
        for d in (1, 2, 3):
            arrived(ref.at[pl.ds(((g + 4 - d) % GROUPS) * CAP, CAP)], ad_rs.at[n, d])

    def adapters_share(n, ref):
        send(ref.at[0], ref.at[2], cp_ss.at[n, 0], cp_rs.at[n, 2], to_partner)
        send(ref.at[0], ref.at[1], cp_ss.at[n, 1], cp_rs.at[n, 1], to_sibling)

    def down_compact(places):
        adapters_arrived(0, drecv, dsend)
        for j in range(REQUESTS):
            dtmp[2 * j : 2 * j + 2, :] = drecv[places[j]].astype(F32)
        dc[0] = dtmp[...].astype(BF16)
        adapters_share(0, dc)

    def up_compact(places):
        adapters_arrived(1, urecv, usend)
        for j in range(REQUESTS):
            uc[0, j] = urecv[places[j]]
        adapters_share(1, uc)

    def adapters_forward(n, ref):
        arrived(ref.at[2], cp_rs.at[n, 2])
        send(ref.at[2], ref.at[3], cp_ss.at[n, 2], cp_rs.at[n, 3], to_sibling)

    def adapters_ready(n, ref):
        arrived(ref.at[1], cp_rs.at[n, 1])
        arrived(ref.at[3], cp_rs.at[n, 3])

    def token_block(r, k):
        return tok[:, r * HALF : (r + 1) * HALF, k * KC : (k + 1) * KC].reshape(HROWS, KC)

    def base(r, k):
        block = token_block(r, k)
        for m in range(4):
            term = jnp.dot(block, wbuf[m, k * KC : (k + 1) * KC, :], preferred_element_type=F32)
            if k == 0:
                acc[r, m] = term
            else:
                acc[r, m] += term

    def low_rank(r, k):
        rows = dc[:, :, k * KC : (k + 1) * KC].reshape(4 * 2 * REQUESTS, KC)
        term = lax.dot_general(
            rows, token_block(r, k), (((1,), (1,)), ((), ())), preferred_element_type=F32
        )
        if k == 0:
            part[r] = term
        else:
            part[r] += term

    ends = []
    total = jnp.int32(0)
    for j in range(REQUESTS):
        total = total + len_ref[g, j]
        ends.append(total)

    def request_of(row, r):
        position = side * 1024 + (row // HALF) * 128 + c * SHARD + r * HALF + row % HALF
        request = jnp.zeros(row.shape, jnp.int32)
        for j in range(REQUESTS):
            request = request + jnp.where(position >= ends[j], 1, 0)
        return request

    z_low = jnp.minimum(z, z_partner)
    quad = z_low * 4 + x

    def codes_send(r):
        row = lax.broadcasted_iota(jnp.int32, (128, HROWS), 0)
        request = request_of(lax.broadcasted_iota(jnp.int32, (128, HROWS), 1), r)
        masked = jnp.where(request == (row % 32) // 2, part[r], 0.0).astype(BF16)
        lane = lax.broadcasted_iota(jnp.int32, (16, 128), 1)
        member = lane // 32
        high = jnp.where(z == z_low, member // 2, 1 - member // 2)
        core = jnp.where(c == 0, member % 2, 1 - member % 2)
        place = high * 4 + core * 2 + lane % 2
        pick = jnp.where(place == lax.broadcasted_iota(jnp.int32, (16, 128), 0), 1.0, 0.0)
        codes = jnp.dot(pick.astype(BF16), masked, preferred_element_type=F32)
        shr[r, quad] = codes[:8]
        for n, dev in enumerate(near):
            cls = (RIGHT, LEFT, FAR, ACROSS, ACROSS_RIGHT, ACROSS_LEFT, ACROSS_FAR)[n]
            send(shr.at[r, quad], shr.at[r, quad], sh_ss.at[r, n], sh_rs.at[r, cls], dev)

    def out_piece(zz, cc, r):
        return out_hbm.at[zz // 2, :, cc, pl.ds(r * HALF, HALF), :]

    def out_local(r):
        return pltpu.make_async_copy(ost.at[r, 0], out_piece(z, c, r), loc_sem.at[3 + r])

    def finish(r):
        z_other_low = 1 - z_low
        quad_low, quad_other = z_low * 4, z_other_low * 4
        for cls, q in (
            (LEFT, quad_low + left), (RIGHT, quad_low + right), (FAR, quad_low + far),
            (ACROSS, quad_other + x), (ACROSS_LEFT, quad_other + left),
            (ACROSS_RIGHT, quad_other + right), (ACROSS_FAR, quad_other + far),
        ):
            arrived(shr.at[r, q], sh_rs.at[r, cls])
        place = lax.broadcasted_iota(jnp.int32, (RANK, 128), 0)
        lane = lax.broadcasted_iota(jnp.int32, (RANK, 128), 1) % RANK
        low, xx, rest = place // 32, (place // 8) % 4, place % 8
        zz = jnp.where(rest // 4 == 0, low, 3 - low)
        rank = zz * 16 + xx * 4 + rest % 4
        order = jnp.where(rank == lane, 1.0, 0.0).astype(BF16)
        codes = shr[r].reshape(RANK, HROWS).astype(BF16)
        codes = lax.dot_general(codes, order, (((0,), (0,)), ((), ())), preferred_element_type=F32)
        request = request_of(lax.broadcasted_iota(jnp.int32, (HROWS, 128), 0), r)
        half = lax.broadcasted_iota(jnp.int32, (HROWS, 128), 1) // RANK
        request = request - half
        spread = jnp.concatenate(
            [jnp.where(request == 2 * b, codes, 0.0).astype(BF16) for b in range(REQUESTS // 2)],
            axis=1,
        )
        for m in (2, 3, 1, 0):
            table = uc[m].reshape(REQUESTS * RANK, COLS)
            update = jnp.dot(spread, table, preferred_element_type=F32)
            result = (acc[r, m] + 0.5 * update).astype(BF16)
            ost[r, m] = result.reshape(SOURCES, HALF, COLS)
            if m == 0:
                out_local(r).start()
            else:
                dev = (None, to_sibling, to_partner, to_partner_other)[m]
                send(ost.at[r, m], out_piece(z, c, r), out_ss.at[r, m], out_rs.at[r, m], dev)

    def out_arrived(r):
        out_local(r).wait()
        arrived(out_piece(z, 1 - c, r), out_rs.at[r, 1])
        arrived(out_piece(z_partner, c, r), out_rs.at[r, 2])
        arrived(out_piece(z_partner, 1 - c, r), out_rs.at[r, 3])

    own_send(0)
    w_own_send(0)
    own_send(1)
    w_sibling_send(0)
    w_sibling_send(1)
    adapters_pick()
    places = request_places()

    def step0():
        w_own_send(1)
        w_first(0)
        w_sibling_send(2)
        w_sibling_send(3)

    def step1():
        w_second(0)
        w_own_send(2)
        w_first(1)
        down_compact(places)

    def step2():
        w_third(0)
        w_second(1)
        w_own_send(3)
        w_first(2)
        up_compact(places)

    def step3():
        w_third(1)
        w_second(2)
        w_ready(0)
        tok_copy.wait()
        base(0, 0)

    def step4():
        w_third(2)
        w_first(3)
        w_ready(1)
        base(0, 1)

    def step5():
        w_second(3)
        adapters_forward(0, dc)
        w_ready(2)
        base(0, 2)

    def step6():
        w_third(3)
        adapters_forward(1, uc)

    def step7():
        w_ready(3)
        base(0, 3)
        adapters_ready(0, dc)
        for k in range(NK):
            low_rank(0, k)
        codes_send(0)
        base(1, 0)
        low_rank(1, 0)
        adapters_ready(1, uc)
        finish(0)

    def step8():
        base(1, 1)
        low_rank(1, 1)
        base(1, 2)
        low_rank(1, 2)

    def step9():
        low_rank(1, 3)
        codes_send(1)
        base(1, 3)
        finish(1)

    steps = [step0, step1, step2, step3, step4, step5, step6, step7, step8, step9]
    for p in range(PIECES + 2):
        if p + 2 < PIECES:
            own_send(p + 2)
        if p < PIECES:
            tok_first(p)
        if 0 <= p - 1 < PIECES:
            tok_second(p - 1)
        if 0 <= p - 2 < PIECES:
            tok_third(p - 2)
        steps[p]()
    for r in range(HALVES):
        out_arrived(r)
    for copy in sends:
        copy.wait_send()


def local(tokens, weight, down, up, lengths, request_adapter_id, adapter_storage_slot):
    dma = pltpu.SemaphoreType.DMA
    any_space = pl.BlockSpec(memory_space=pl.ANY)
    smem = pl.BlockSpec(memory_space=pltpu.SMEM)
    slots = GROUPS * CAP
    out = pl.pallas_call(
        kernel,
        out_shape=jax.ShapeDtypeStruct((2, SOURCES, 2, SHARD, COLS), BF16),
        in_specs=[any_space] * 4 + [smem] * 3,
        out_specs=any_space,
        scratch_shapes=[
            pltpu.VMEM((SOURCES, SHARD, WIDTH), BF16),
            pltpu.VMEM((4, WIDTH, COLS), BF16),
            pltpu.VMEM((OWNED, 2, WIDTH), BF16),
            pltpu.VMEM((OWNED, RANK, COLS), BF16),
            pltpu.VMEM((slots, 2, WIDTH), BF16),
            pltpu.VMEM((slots, RANK, COLS), BF16),
            pltpu.VMEM((slots, 2, WIDTH), BF16),
            pltpu.VMEM((slots, RANK, COLS), BF16),
            pltpu.VMEM((2 * REQUESTS, WIDTH), F32),
            pltpu.VMEM((4, 2 * REQUESTS, WIDTH), BF16),
            pltpu.VMEM((4, REQUESTS, RANK, COLS), BF16),
            pltpu.VMEM((HALVES, 4, HROWS, COLS), F32),
            pltpu.VMEM((HALVES, 8 * REQUESTS, HROWS), F32),
            pltpu.VMEM((HALVES, SOURCES, 8, HROWS), F32),
            pltpu.VMEM((HALVES, 4, SOURCES, HALF, COLS), BF16),
            dma((5,)),
            dma((NK,)),
            dma((7, PIECES)),
            dma((7, PIECES)),
            dma((4, NK)),
            dma((4, NK)),
            dma((NK,)),
            dma((NK,)),
            dma((4, NK)),
            dma((4, NK)),
            dma((2, 4)),
            dma((2, 4)),
            dma((2, 3)),
            dma((2, 4)),
            dma((HALVES, 7)),
            dma((HALVES, 7)),
            dma((HALVES, 4)),
            dma((HALVES, 4)),
        ],
        compiler_params=pltpu.CompilerParams(
            collective_id=0, has_side_effects=True, vmem_limit_bytes=60 * 1024 * 1024
        ),
    )(tokens, weight, down, up, lengths, request_adapter_id, adapter_storage_slot)
    return out.reshape(2 * SOURCES * 2 * SHARD, COLS)


def solution(mesh):
    placed = (
        P(("group", "tp"), None),
        P(None, "tp"),
        P("group", "tp", None),
        P("group", None, "tp"),
        P(),
        P(),
        P(),
    )
    return jax.shard_map(
        local, mesh=mesh, in_specs=placed, out_specs=P("group", "tp"), check_vma=False
    )
```

time: 283 us -> 112 us (0.40)
  Pallas kernels: 0 us -> 109 us
  waiting for transfers between devices: 99.6 us -> 0 us
  matrix products: 63.9 us -> 0 us
  local copies, waits for them, and re-layouts: 65.3 us -> 2.26 us
  blocking collectives: 24.6 us -> 0 us
  between operations: 13.5 us -> 0.01 us
  starting transfers between devices: 8.51 us -> 0 us
  other arithmetic: 6.72 us -> 0 us
    pallas_call x0 -> x1, Pallas kernels: none -> 109 us  [local(): pl.pallas_call(kernel, out_shape=jax.ShapeDtypeStruct((2, SOURCES, 2, SHA...]
    all_gather x1 -> x0, waiting for transfers between devices: 92 us -> none  [local(): gathered = lax.all_gather(tokens, 'tp', axis=0, tiled=True)]
    dot_general x6 -> x0, matrix products: 63.9 us -> none  [the longest x4 32.3 us: up_block(): jnp.einsum('tr,trc->tc', codes_block, b_tokens, preferred_element_type=jn...]
    gather x6 -> x0, local copies, waits for them, and re-layouts: 59.7 us -> none  [the longest x4 52.4 us: up_block(): b_tokens = b_table[slots_block]]
    all_gather x1 -> x0, blocking collectives: 24.6 us -> none  [local(): shrink = lax.all_gather(shrink_part, 'tp', axis=1, tiled=True)]
    all_to_all x2 -> x0, starting transfers between devices: 8.51 us -> none  [the longest x1 5.01 us: fetch_pieces(): lax.all_to_all(down_token_rows, 'group', split_axis=0, concat_axis=0, til...]
    all_to_all x2 -> x0, waiting for transfers between devices: 6.88 us -> none  [the longest x1 6.88 us: fetch_pieces(): lax.all_to_all(down_token_rows, 'group', split_axis=0, concat_axis=0, til...]
    dynamic_update_slice x4 -> x0, local copies, waits for them, and re-layouts: 3.37 us -> none  [local(): lax.map(up_block, (shrink.reshape(block_count, block_rows, full_rank_outp...]
  transfers between devices with their start and end apart: 3 -> 0, of which waited for: 2 -> 0; matrix products, arithmetic and copies ran while one was open for 10% -> 0% of each run, Pallas kernels for 0% -> 0%
where the time goes in v1:
time: 112 us
  Pallas kernels  109 us (97%)
  local copies, waits for them, and re-layouts  2.26 us (2%)
    pallas_call x1, Pallas kernels, local(): pl.pallas_call(kernel, out_shape=jax.ShapeDtypeStruct((2, SOURCES, 2, SHA...  109 us
    unnamed x1, local copies, waits for them, and re-layouts  2.26 us

profile of v1, /device:TPU:1, one launch (start us, length us, event | category | flops | bytes accessed | tf_op | source)
XLA Modules:
  0.0 111.8 jit_solution(13741169365844307251)
XLA Ops:
  0.0 109.5 %shard_map.73 = bf16[2,8,2,64,256]{4,3,2,1,0:T(8,128)(2,1)} custom-call(bf16[64,8192]{1,0:T(8,128)(2,1)} %tok_hbm.1, bf16[8192,256]{1,0:T(8,128)(2,1)} %w_hbm.1, bf16[128,2,8192]{2,1,0:T(2,128)(2,1)} %down_hbm.1, bf16[128,64,256]{2,1,0:T(8,128)(2,1)} %up_hbm.1, s32[4,16]{1,0:T(4,128)} %len_ref.1, s32[4,16]{1,0:T(4,128)} %rid_ref.1, s32[512]{0:T(512)} %slot_ref.1), custom_call_target="tpu_custom_call" | custom-call | tf_op jit(solution)/shard_map/pallas_call | solution.py:476
  109.5 2.3 %copy.9 = bf16[2048,256]{1,0:T(8,128)(2,1)} copy(bf16[2048,256]{1,0:T(8,128)(2,1)} %bitcast.1) | data formatting | bytes 2097152

commit v2 on v1

v2 whole, which is shorter than its diff:
```python
import jax
import jax.numpy as jnp
from jax import lax
from jax.experimental import pallas as pl
from jax.experimental.pallas import tpu as pltpu
from jax.sharding import PartitionSpec as P

MESH = pl.DeviceIdType.MESH
F32 = jnp.float32
BF16 = jnp.bfloat16

CAP = 6
GROUPS = 4
REQUESTS = 16
RANK = 64
WIDTH = 8192
COLS = 256
SHARD = 64
PART = (48, 16)
START = (0, 48)
PARTS = len(PART)
LANES = 128
HALVES = COLS // LANES
SOURCES = 8
NK = 4
KC = WIDTH // NK
WC = KC // 4
PIECES = PARTS * NK
CHUNKS = HALVES * NK
OWNED = 128
W_FAR_DIRECT = (6, 7)

LEFT, RIGHT, FAR, ACROSS, ACROSS_LEFT, ACROSS_RIGHT, ACROSS_FAR = range(7)


def kernel(
    tok_hbm, w_hbm, down_hbm, up_hbm, len_ref, rid_ref, slot_ref, out_hbm,
    tok, wbuf, dloc, uloc, dsend, usend, drecv, urecv, dtmp, dc, uc,
    acc0, acc1, part0, part1, shr0, shr1, spread0, spread1, ost0, ost1,
    loc_sem, own_sem, tok_ss, tok_rs, w_ss, w_rs, ws_ss, ws_rs, wf_ss, wf_rs,
    ad_ss, ad_rs, cp_ss, cp_rs, sh_ss, sh_rs, out_ss, out_rs,
):
    acc, part, shr = (acc0, acc1), (part0, part1), (shr0, shr1)
    spread, ost = (spread0, spread1), (ost0, ost1)
    g = lax.axis_index("group")
    tp = lax.axis_index("tp")
    z = tp // 8
    x = (tp // 2) % 4
    c = tp % 2
    side = z // 2
    bit = z % 2
    z_across = 2 * side + 1 - bit
    z_partner = 3 - z

    def device(zz, xx, cc, gg=None):
        return (g if gg is None else gg, (zz * 4 + xx) * 2 + cc)

    left, right, far = (x + 3) % 4, (x + 1) % 4, (x + 2) % 4
    to_left, to_right = device(z, left, c), device(z, right, c)
    to_across = device(z_across, x, c)
    to_sibling = device(z, x, 1 - c)
    to_partner = device(z_partner, x, c)
    to_partner_other = device(z_partner, x, 1 - c)

    sends = []

    def send(src, dst, ss, rs, dev):
        copy = pltpu.make_async_remote_copy(
            src_ref=src, dst_ref=dst, send_sem=ss, recv_sem=rs, device_id=dev, device_id_type=MESH
        )
        copy.start()
        sends.append(copy)

    waited = set()

    def arrived(key, dst, rs):
        if key not in waited:
            waited.add(key)
            pltpu.make_async_copy(dst, dst, rs).wait()

    def once(key, copy):
        if key not in waited:
            waited.add(key)
            copy.wait()

    down_copy = pltpu.make_async_copy(down_hbm, dloc, loc_sem.at[0])
    up_copy = pltpu.make_async_copy(up_hbm, uloc, loc_sem.at[1])
    mine = bit * 4 + x
    tok_copy = pltpu.make_async_copy(tok_hbm, tok.at[mine], loc_sem.at[2])
    def w_at(m, i, start, rows):
        h, k = divmod(i, NK)
        return wbuf.at[h, pl.ds(k * KC + start, rows), pl.ds(m * LANES, LANES)]

    def w_own_at(i, start, rows):
        h, k = divmod(i, NK)
        return w_hbm.at[pl.ds(k * KC + start, rows), pl.ds(h * LANES, LANES)]

    w_copies = [
        pltpu.make_async_copy(w_own_at(i, 0, KC), w_at(0, i, 0, KC), own_sem.at[i])
        for i in range(CHUNKS)
    ]
    down_copy.start()
    up_copy.start()
    tok_copy.start()
    for copy in w_copies:
        copy.start()

    peers = [device(z, xx, c) for xx in (left, right, far)]
    peers += [device(z_across, xx, c) for xx in (x, left, right, far)]
    near = list(peers)
    peers += [to_sibling, to_partner, to_partner_other]
    peers += [device(z, x, c, (g + d) % GROUPS) for d in (1, 2, 3)]
    barrier = pltpu.get_barrier_semaphore()
    for dev in peers:
        pl.semaphore_signal(barrier, inc=1, device_id=dev, device_id_type=MESH)
    pl.semaphore_wait(barrier, len(peers))

    def at(source, p):
        r, k = divmod(p, NK)
        return tok.at[source, pl.ds(START[r], PART[r]), pl.ds(k * KC, KC)]

    def tok_send(source, p, n, cls, dev):
        send(at(source, p), at(source, p), tok_ss.at[n, p], tok_rs.at[cls, p], dev)

    s_left, s_right, s_far = bit * 4 + left, bit * 4 + right, bit * 4 + far
    other = (1 - bit) * 4
    a_mine, a_left, a_right, a_far = other + x, other + left, other + right, other + far

    def across_first(p):
        return p % 2 == 0

    def relay_right(p):
        return (p // 2) % 2 == 0

    sources = {
        LEFT: s_left, RIGHT: s_right, FAR: s_far, ACROSS: a_mine,
        ACROSS_LEFT: a_left, ACROSS_RIGHT: a_right, ACROSS_FAR: a_far,
    }

    def tok_arrived(cls, p):
        arrived(("tok", cls, p), at(sources[cls], p), tok_rs.at[cls, p])

    def own_piece(p):
        r, k = divmod(p, NK)
        return tok_hbm.at[pl.ds(START[r], PART[r]), pl.ds(k * KC, KC)]

    def own_across(p):
        send(own_piece(p), at(mine, p), tok_ss.at[0, p], tok_rs.at[ACROSS, p], to_across)

    def own_sides(p):
        send(own_piece(p), at(mine, p), tok_ss.at[1, p], tok_rs.at[LEFT, p], to_right)
        send(own_piece(p), at(mine, p), tok_ss.at[2, p], tok_rs.at[RIGHT, p], to_left)

    def pass_across(p):
        tok_arrived(ACROSS, p)
        tok_send(a_mine, p, 3, ACROSS_LEFT, to_right)
        tok_send(a_mine, p, 4, ACROSS_RIGHT, to_left)

    def pass_left(p):
        tok_arrived(LEFT, p)
        if relay_right(p):
            tok_send(s_left, p, 5, FAR, to_right)
        if not across_first(p):
            tok_send(s_left, p, 3, ACROSS_LEFT, to_across)

    def pass_right(p):
        tok_arrived(RIGHT, p)
        if not relay_right(p):
            tok_send(s_right, p, 5, FAR, to_left)
        if not across_first(p):
            tok_send(s_right, p, 4, ACROSS_RIGHT, to_across)

    def pass_far(p):
        tok_arrived(FAR, p)
        tok_send(s_far, p, 6, ACROSS_FAR, to_across)

    def pass_across_left(p):
        tok_arrived(ACROSS_LEFT, p)
        tok_send(a_left, p, 6, ACROSS_FAR, to_right)

    def pass_across_right(p):
        tok_arrived(ACROSS_RIGHT, p)
        tok_send(a_right, p, 6, ACROSS_FAR, to_left)

    def tok_ready(r, k):
        once("own tokens", tok_copy)
        for cls in sources:
            tok_arrived(cls, r * NK + k)

    g_next, g_prev, g_far = (g + 1) % GROUPS, (g + 3) % GROUPS, (g + 2) % GROUPS
    to_next, to_prev = device(z, x, c, g_next), device(z, x, c, g_prev)
    w_quarters = (g, g_prev, g_far, g_next)

    def w_own(i):
        src, dst = w_own_at(i, g * WC, WC), w_at(2, i, g * WC, WC)
        send(src, dst, w_ss.at[0, i], w_rs.at[0, i], to_partner)

    def w_own_far(i):
        src, dst = w_own_at(i, g_far * WC, WC), w_at(2, i, g_far * WC, WC)
        send(src, dst, w_ss.at[3, i], w_rs.at[2, i], to_partner)

    def w_sibling(i):
        src, dst = w_own_at(i, 0, KC), w_at(1, i, 0, KC)
        send(src, dst, ws_ss.at[i], ws_rs.at[i], to_sibling)

    def w_arrived(cls, i):
        arrived(("w", cls, i), w_at(2, i, w_quarters[cls] * WC, WC), w_rs.at[cls, i])

    def w_forward(i, cls):
        start = w_quarters[cls] * WC
        src, dst = w_at(2, i, start, WC), w_at(3, i, start, WC)
        send(src, dst, wf_ss.at[cls, i], wf_rs.at[cls, i], to_sibling)

    def w_send(i, q, n, cls, dev):
        ref = w_at(2, i, q * WC, WC)
        send(ref, ref, w_ss.at[n, i], w_rs.at[cls, i], dev)

    def w_pass(i):
        w_arrived(0, i)
        w_send(i, g, 1, 1, to_next)
        w_send(i, g, 2, 3, to_prev)
        w_forward(i, 0)

    def w_pass_prev(i):
        w_arrived(1, i)
        if i not in W_FAR_DIRECT and i % 2 == 0:
            w_send(i, g_prev, 3, 2, to_next)
        w_forward(i, 1)

    def w_pass_next(i):
        w_arrived(3, i)
        if i not in W_FAR_DIRECT and i % 2 == 1:
            w_send(i, g_next, 3, 2, to_prev)
        w_forward(i, 3)

    def w_pass_far(i):
        w_arrived(2, i)
        w_forward(i, 2)

    def w_ready(i):
        once(("own w", i), w_copies[i])
        arrived(("sibling w", i), w_at(1, i, 0, KC), ws_rs.at[i])
        for cls, q in enumerate(w_quarters):
            arrived(("other w", cls, i), w_at(3, i, q * WC, WC), wf_rs.at[cls, i])

    def picked_places():
        picked = []
        for dest in range(GROUPS):
            index = [jnp.int32(0)] * CAP
            count = jnp.int32(0)
            for j in range(REQUESTS):
                slot = slot_ref[rid_ref[dest, j]]
                is_mine = slot // OWNED == g
                local = slot % OWNED
                for p in range(min(CAP, j + 1)):
                    index[p] = jnp.where(is_mine & (count == p), local, index[p])
                count = count + is_mine.astype(jnp.int32)
            picked += index
        return picked

    def adapters_send(n, table, picks, gets):
        for p in range(GROUPS * CAP):
            picks[p] = table[picked[p]]
        for d in (1, 3, 2):
            rows = pl.ds(((g + d) % GROUPS) * CAP, CAP)
            dev = device(z, x, c, (g + d) % GROUPS)
            send(picks.at[rows], gets.at[pl.ds(g * CAP, CAP)], ad_ss.at[n, d], ad_rs.at[n, d], dev)
        rows = pl.ds(g * CAP, CAP)
        pltpu.make_async_copy(picks.at[rows], gets.at[rows], ad_ss.at[n, 0]).start()

    def down_pick():
        down_copy.wait()
        adapters_send(0, dloc, dsend, drecv)

    def up_pick():
        up_copy.wait()
        adapters_send(1, uloc, usend, urecv)

    def request_places():
        places = []
        counts = [jnp.int32(0)] * GROUPS
        for j in range(REQUESTS):
            owner = slot_ref[rid_ref[g, j]] // OWNED
            place = jnp.int32(0)
            for o in range(GROUPS):
                hit = owner == o
                place = place + jnp.where(hit, o * CAP + counts[o], 0)
                counts[o] = counts[o] + hit.astype(jnp.int32)
            places.append(place)
        return places

    def adapters_arrived(n, ref, src):
        rows = pl.ds(g * CAP, CAP)
        pltpu.make_async_copy(src.at[rows], ref.at[rows], ad_ss.at[n, 0]).wait()
        for d in (1, 2, 3):
            rows = pl.ds(((g + 4 - d) % GROUPS) * CAP, CAP)
            arrived(("picked", n, d), ref.at[rows], ad_rs.at[n, d])

    def adapters_share(n, ref):
        send(ref.at[0], ref.at[2], cp_ss.at[n, 0], cp_rs.at[n, 2], to_partner)
        send(ref.at[0], ref.at[1], cp_ss.at[n, 1], cp_rs.at[n, 1], to_sibling)

    def down_compact():
        adapters_arrived(0, drecv, dsend)
        for j in range(REQUESTS):
            dtmp[2 * j : 2 * j + 2, :] = drecv[places[j]].astype(F32)
        dc[0] = dtmp[...].astype(BF16)
        adapters_share(0, dc)

    def up_compact():
        adapters_arrived(1, urecv, usend)
        for j in range(REQUESTS):
            uc[0, j] = urecv[places[j]]
        adapters_share(1, uc)

    def down_forward():
        adapters_forward(0, dc)

    def up_forward():
        adapters_forward(1, uc)

    def adapters_forward(n, ref):
        arrived(("adapters", n, 2), ref.at[2], cp_rs.at[n, 2])
        send(ref.at[2], ref.at[3], cp_ss.at[n, 2], cp_rs.at[n, 3], to_sibling)

    def adapters_ready(n, ref):
        arrived(("adapters", n, 1), ref.at[1], cp_rs.at[n, 1])
        arrived(("adapters", n, 3), ref.at[3], cp_rs.at[n, 3])

    begun = set()

    def add(key, ref, term):
        if key in begun:
            ref[...] += term
        else:
            begun.add(key)
            ref[...] = term

    def token_block(r, k):
        rows = tok[:, START[r] : START[r] + PART[r], k * KC : (k + 1) * KC]
        return rows.reshape(SOURCES * PART[r], KC)

    def base(r, k, h):
        tok_ready(r, k)
        w_ready(h * NK + k)
        weight = wbuf[h, k * KC : (k + 1) * KC, :]
        term = jnp.dot(token_block(r, k), weight, preferred_element_type=F32)
        add(("base", r, h), acc[r].at[h], term)

    def low_rank(r, k):
        tok_ready(r, k)
        adapters_ready(0, dc)
        rows = dc[:, :, k * KC : (k + 1) * KC].reshape(4 * 2 * REQUESTS, KC)
        term = lax.dot_general(
            rows, token_block(r, k), (((1,), (1,)), ((), ())), preferred_element_type=F32
        )
        add(("low rank", r), part[r], term)

    ends = []
    total = jnp.int32(0)
    for j in range(REQUESTS):
        total = total + len_ref[g, j]
        ends.append(total)

    def request_of(row, r):
        source = jnp.zeros(row.shape, jnp.int32)
        for n in range(1, SOURCES):
            source = source + jnp.where(row >= n * PART[r], 1, 0)
        position = side * 1024 + source * 128 + c * SHARD + START[r] + row - source * PART[r]
        request = jnp.zeros(row.shape, jnp.int32)
        for j in range(REQUESTS):
            request = request + jnp.where(position >= ends[j], 1, 0)
        return request

    z_low = jnp.minimum(z, z_partner)
    quad = z_low * 4 + x

    def codes_send(r):
        shape = (8 * REQUESTS, SOURCES * PART[r])
        row = lax.broadcasted_iota(jnp.int32, shape, 0)
        request = request_of(lax.broadcasted_iota(jnp.int32, shape, 1), r)
        masked = jnp.where(request == (row % 32) // 2, part[r][...], 0.0).astype(BF16)
        lane = lax.broadcasted_iota(jnp.int32, (16, 128), 1)
        member = lane // 32
        high = jnp.where(z == z_low, member // 2, 1 - member // 2)
        core = jnp.where(c == 0, member % 2, 1 - member % 2)
        place = high * 4 + core * 2 + lane % 2
        pick = jnp.where(place == lax.broadcasted_iota(jnp.int32, (16, 128), 0), 1.0, 0.0)
        codes = jnp.dot(pick.astype(BF16), masked, preferred_element_type=F32)
        shr[r][quad] = codes[:8]
        for n, dev in enumerate(near):
            cls = (RIGHT, LEFT, FAR, ACROSS, ACROSS_RIGHT, ACROSS_LEFT, ACROSS_FAR)[n]
            ref = shr[r].at[quad]
            send(ref, ref, sh_ss.at[r, n], sh_rs.at[r, cls], dev)

    def out_piece(zz, cc, r, h):
        rows, lanes = pl.ds(START[r], PART[r]), pl.ds(h * LANES, LANES)
        return out_hbm.at[zz // 2, :, cc, rows, lanes]

    def out_local(r, h):
        sem = loc_sem.at[3 + r * HALVES + h]
        return pltpu.make_async_copy(ost[r].at[h, 0], out_piece(z, c, r, h), sem)

    def codes_spread(r):
        z_other_low = 1 - z_low
        quad_low, quad_other = z_low * 4, z_other_low * 4
        for cls, q in (
            (LEFT, quad_low + left), (RIGHT, quad_low + right), (FAR, quad_low + far),
            (ACROSS, quad_other + x), (ACROSS_LEFT, quad_other + left),
            (ACROSS_RIGHT, quad_other + right), (ACROSS_FAR, quad_other + far),
        ):
            arrived(("codes", r, cls), shr[r].at[q], sh_rs.at[r, cls])
        place = lax.broadcasted_iota(jnp.int32, (RANK, 128), 0)
        lane = lax.broadcasted_iota(jnp.int32, (RANK, 128), 1) % RANK
        low, xx, rest = place // 32, (place // 8) % 4, place % 8
        zz = jnp.where(rest // 4 == 0, low, 3 - low)
        rank = zz * 16 + xx * 4 + rest % 4
        order = jnp.where(rank == lane, 1.0, 0.0).astype(BF16)
        hrows = SOURCES * PART[r]
        codes = shr[r][...].reshape(RANK, hrows).astype(BF16)
        codes = lax.dot_general(codes, order, (((0,), (0,)), ((), ())), preferred_element_type=F32)
        request = request_of(lax.broadcasted_iota(jnp.int32, (hrows, 128), 0), r)
        half = lax.broadcasted_iota(jnp.int32, (hrows, 128), 1) // RANK
        request = request - half
        for b in range(REQUESTS // 2):
            block = jnp.where(request == 2 * b, codes, 0.0).astype(BF16)
            spread[r][:, b * 128 : (b + 1) * 128] = block

    def finish(r, h):
        adapters_ready(1, uc)
        lanes = slice(h * LANES, (h + 1) * LANES)
        for pair in (1, 0):
            table = jnp.concatenate(
                [uc[m, :, :, lanes].reshape(REQUESTS * RANK, LANES) for m in (2 * pair, 2 * pair + 1)],
                axis=1,
            )
            update = jnp.dot(spread[r][...], table, preferred_element_type=F32)
            base_sum = acc[r][h, :, pair * 2 * LANES : (pair + 1) * 2 * LANES]
            result = (base_sum + 0.5 * update).astype(BF16)
            for n in (0, 1):
                m = 2 * pair + n
                piece = result[:, n * LANES : (n + 1) * LANES]
                ost[r][h, m] = piece.reshape(SOURCES, PART[r], LANES)
                if m == 0:
                    out_local(r, h).start()
                else:
                    dev = (None, to_sibling, to_partner, to_partner_other)[m]
                    ss, rs = out_ss.at[r, h, m], out_rs.at[r, h, m]
                    send(ost[r].at[h, m], out_piece(z, c, r, h), ss, rs, dev)

    def out_arrived(r, h):
        out_local(r, h).wait()
        for m, (zz, cc) in enumerate(((z, 1 - c), (z_partner, c), (z_partner, 1 - c)), 1):
            arrived(("out", r, h, m), out_piece(zz, cc, r, h), out_rs.at[r, h, m])

    picked = picked_places()
    places = request_places()

    order = [
        (w_own, 4), (w_sibling, 4), (w_own, 6), (own_across, 0), (own_sides, 0), (w_sibling, 0),
        (w_sibling, 1), (w_own_far, 6), (w_own, 0), (w_own_far, 7), (w_sibling, 3), (w_sibling, 7),
        (w_sibling, 2), (w_own, 7), (own_across, 1), (w_own, 5), (w_own, 3), (w_own, 2),
        (own_sides, 1), (own_sides, 2), (own_across, 2), (w_sibling, 6), (w_own, 1), (w_sibling, 5),
        (down_pick,), (own_sides, 3), (own_across, 3), (pass_left, 0), (w_pass, 4), (up_pick,),
        (pass_across, 0), (w_pass_far, 6), (own_across, 4), (pass_left, 1), (pass_right, 1),
        (pass_across, 2), (pass_right, 2), (down_compact,), (w_pass_far, 7), (w_pass, 0),
        (w_pass_prev, 4), (w_pass_next, 4), (pass_left, 3), (pass_right, 3), (pass_across, 4),
        (w_pass, 5), (w_pass, 7), (up_compact,), (pass_across_right, 2), (pass_across_left, 0),
        (own_across, 5), (w_pass, 2), (w_pass_prev, 0), (w_pass_next, 0), (own_across, 6),
        (own_across, 7), (pass_far, 1), (w_pass_far, 4), (w_pass_next, 5), (own_sides, 4),
        (own_sides, 5), (w_pass, 6), (w_pass_prev, 5), (w_pass_next, 7), (own_sides, 6),
        (pass_far, 3), (own_sides, 7), (pass_across_left, 4), (w_pass, 1), (w_pass_prev, 7),
        (w_pass_next, 2), (pass_across, 6), (w_pass, 3), (w_pass_far, 5), (down_forward,),
        (w_pass_prev, 2), (base, 0, 0, 1), (pass_left, 4), (w_pass_far, 0), (low_rank, 0, 2),
        (w_pass_next, 6), (pass_left, 5), (pass_right, 5), (low_rank, 0, 0), (base, 0, 0, 0),
        (base, 0, 1, 1), (w_pass_prev, 6), (pass_right, 6), (w_pass_next, 1), (pass_left, 7),
        (pass_right, 7), (low_rank, 0, 1), (base, 0, 2, 1), (pass_across_right, 6),
        (w_pass_prev, 1), (w_pass_next, 3), (low_rank, 0, 3), (base, 0, 3, 1), (codes_send, 0),
        (base, 1, 0, 1), (pass_far, 7), (low_rank, 1, 0), (up_forward,), (base, 1, 0, 0),
        (pass_far, 5), (base, 1, 2, 1), (low_rank, 1, 2), (w_pass_prev, 3), (codes_spread, 0),
        (w_pass_far, 1), (finish, 0, 1), (w_pass_far, 2), (w_pass_far, 3), (base, 0, 1, 0),
        (base, 1, 3, 1), (low_rank, 1, 3), (base, 0, 2, 0), (base, 0, 3, 0), (finish, 0, 0),
        (low_rank, 1, 1), (codes_send, 1), (base, 1, 1, 0), (base, 1, 1, 1), (base, 1, 3, 0),
        (base, 1, 2, 0), (codes_spread, 1), (finish, 1, 1), (finish, 1, 0),
    ]
    for action, *args in order:
        action(*args)
    for r in range(PARTS):
        for h in range(HALVES):
            out_arrived(r, h)
    for copy in sends:
        copy.wait_send()


def local(tokens, weight, down, up, lengths, request_adapter_id, adapter_storage_slot):
    dma = pltpu.SemaphoreType.DMA
    any_space = pl.BlockSpec(memory_space=pl.ANY)
    smem = pl.BlockSpec(memory_space=pltpu.SMEM)
    slots = GROUPS * CAP
    out = pl.pallas_call(
        kernel,
        out_shape=jax.ShapeDtypeStruct((2, SOURCES, 2, SHARD, COLS), BF16),
        in_specs=[any_space] * 4 + [smem] * 3,
        out_specs=any_space,
        scratch_shapes=[
            pltpu.VMEM((SOURCES, SHARD, WIDTH), BF16),
            pltpu.VMEM((HALVES, WIDTH, 4 * LANES), BF16),
            pltpu.VMEM((OWNED, 2, WIDTH), BF16),
            pltpu.VMEM((OWNED, RANK, COLS), BF16),
            pltpu.VMEM((slots, 2, WIDTH), BF16),
            pltpu.VMEM((slots, RANK, COLS), BF16),
            pltpu.VMEM((slots, 2, WIDTH), BF16),
            pltpu.VMEM((slots, RANK, COLS), BF16),
            pltpu.VMEM((2 * REQUESTS, WIDTH), F32),
            pltpu.VMEM((4, 2 * REQUESTS, WIDTH), BF16),
            pltpu.VMEM((4, REQUESTS, RANK, COLS), BF16),
            *(pltpu.VMEM((HALVES, SOURCES * n, 4 * LANES), F32) for n in PART),
            *(pltpu.VMEM((8 * REQUESTS, SOURCES * n), F32) for n in PART),
            *(pltpu.VMEM((SOURCES, 8, SOURCES * n), F32) for n in PART),
            *(pltpu.VMEM((SOURCES * n, REQUESTS * RANK), BF16) for n in PART),
            *(pltpu.VMEM((HALVES, 4, SOURCES, n, LANES), BF16) for n in PART),
            dma((3 + PARTS * HALVES,)),
            dma((CHUNKS,)),
            dma((7, PIECES)),
            dma((7, PIECES)),
            dma((4, CHUNKS)),
            dma((4, CHUNKS)),
            dma((CHUNKS,)),
            dma((CHUNKS,)),
            dma((4, CHUNKS)),
            dma((4, CHUNKS)),
            dma((2, 4)),
            dma((2, 4)),
            dma((2, 3)),
            dma((2, 4)),
            dma((PARTS, 7)),
            dma((PARTS, 7)),
            dma((PARTS, HALVES, 4)),
            dma((PARTS, HALVES, 4)),
        ],
        compiler_params=pltpu.CompilerParams(
            collective_id=0, has_side_effects=True, vmem_limit_bytes=60 * 1024 * 1024
        ),
    )(tokens, weight, down, up, lengths, request_adapter_id, adapter_storage_slot)
    return out.reshape(2 * SOURCES * 2 * SHARD, COLS)


def solution(mesh):
    placed = (
        P(("group", "tp"), None),
        P(None, "tp"),
        P("group", "tp", None),
        P("group", None, "tp"),
        P(),
        P(),
        P(),
    )
    return jax.shard_map(
        local, mesh=mesh, in_specs=placed, out_specs=P("group", "tp"), check_vma=False
    )
```

time: 112 us -> 87.7 us (0.78)
  Pallas kernels: 109 us -> 85.3 us
    pallas_call x1, Pallas kernels: 109 us -> 85.3 us  [local(): pl.pallas_call(kernel, out_shape=jax.ShapeDtypeStruct((2, SOURCES, 2, SHA...]
where the time goes in v2:
time: 87.7 us; the launch traced here: 87.5 us
  Pallas kernels  85.3 us (97%)
  local copies, waits for them, and re-layouts  2.26 us (3%)
    pallas_call x1, Pallas kernels, local(): pl.pallas_call(kernel, out_shape=jax.ShapeDtypeStruct((2, SOURCES, 2, SHA...  85.3 us
    unnamed x1, local copies, waits for them, and re-layouts  2.26 us

profile of v2, /device:TPU:1, one launch (start us, length us, event | category | flops | bytes accessed | tf_op | source)
XLA Modules:
  0.0 87.5 jit_solution(325226680039128010)
XLA Ops:
  0.0 85.3 %shard_map.73 = bf16[2,8,2,64,256]{4,3,2,1,0:T(8,128)(2,1)} custom-call(bf16[64,8192]{1,0:T(8,128)(2,1)} %tok_hbm.1, bf16[8192,256]{1,0:T(8,128)(2,1)} %w_hbm.1, bf16[128,2,8192]{2,1,0:T(2,128)(2,1)} %down_hbm.1, bf16[128,64,256]{2,1,0:T(8,128)(2,1)} %up_hbm.1, s32[4,16]{1,0:T(4,128)} %len_ref.1, s32[4,16]{1,0:T(4,128)} %rid_ref.1, s32[512]{0:T(512)} %slot_ref.1), custom_call_target="tpu_custom_call" | custom-call | tf_op jit(solution)/shard_map/pallas_call | solution.py:500
  85.3 2.3 %copy.9 = bf16[2048,256]{1,0:T(8,128)(2,1)} copy(bf16[2048,256]{1,0:T(8,128)(2,1)} %bitcast.1) | data formatting | bytes 2097152

commit v3 on v2

--- a/solution.py
+++ b/solution.py
@@ -22,9 +22,9 @@
 LANES = 128
 HALVES = COLS // LANES
 SOURCES = 8
-NK = 4
-KC = WIDTH // NK
-WC = KC // 4
+KCS = (2304, 1792, 2304, 1792)
+NK = len(KCS)
+KSTART = tuple(sum(KCS[:k]) for k in range(NK))
 PIECES = PARTS * NK
 CHUNKS = HALVES * NK
 OWNED = 128
@@ -64,6 +64,11 @@
 
     sends = []
 
+    def sent():
+        for copy in sends:
+            copy.wait_send()
+        sends.clear()
+
     def send(src, dst, ss, rs, dev):
         copy = pltpu.make_async_remote_copy(
             src_ref=src, dst_ref=dst, send_sem=ss, recv_sem=rs, device_id=dev, device_id_type=MESH
@@ -87,23 +92,25 @@
     up_copy = pltpu.make_async_copy(up_hbm, uloc, loc_sem.at[1])
     mine = bit * 4 + x
     tok_copy = pltpu.make_async_copy(tok_hbm, tok.at[mine], loc_sem.at[2])
-    def w_at(m, i, start, rows):
+    def w_rows(k, quarter):
+        if quarter is None:
+            return pl.ds(KSTART[k], KCS[k])
+        return pl.ds(KSTART[k] + quarter * (KCS[k] // 4), KCS[k] // 4)
+
+    def w_at(m, i, quarter=None):
         h, k = divmod(i, NK)
-        return wbuf.at[h, pl.ds(k * KC + start, rows), pl.ds(m * LANES, LANES)]
-
-    def w_own_at(i, start, rows):
+        return wbuf.at[h, w_rows(k, quarter), pl.ds(m * LANES, LANES)]
+
+    def w_own_at(i, quarter=None):
         h, k = divmod(i, NK)
-        return w_hbm.at[pl.ds(k * KC + start, rows), pl.ds(h * LANES, LANES)]
+        return w_hbm.at[w_rows(k, quarter), pl.ds(h * LANES, LANES)]
 
     w_copies = [
-        pltpu.make_async_copy(w_own_at(i, 0, KC), w_at(0, i, 0, KC), own_sem.at[i])
+        pltpu.make_async_copy(w_own_at(i), w_at(0, i), own_sem.at[i])
         for i in range(CHUNKS)
     ]
     down_copy.start()
     up_copy.start()
-    tok_copy.start()
-    for copy in w_copies:
-        copy.start()
 
     peers = [device(z, xx, c) for xx in (left, right, far)]
     peers += [device(z_across, xx, c) for xx in (x, left, right, far)]
@@ -117,7 +124,7 @@
 
     def at(source, p):
         r, k = divmod(p, NK)
-        return tok.at[source, pl.ds(START[r], PART[r]), pl.ds(k * KC, KC)]
+        return tok.at[source, pl.ds(START[r], PART[r]), pl.ds(KSTART[k], KCS[k])]
 
     def tok_send(source, p, n, cls, dev):
         send(at(source, p), at(source, p), tok_ss.at[n, p], tok_rs.at[cls, p], dev)
@@ -142,7 +149,7 @@
 
     def own_piece(p):
         r, k = divmod(p, NK)
-        return tok_hbm.at[pl.ds(START[r], PART[r]), pl.ds(k * KC, KC)]
+        return tok_hbm.at[pl.ds(START[r], PART[r]), pl.ds(KSTART[k], KCS[k])]
 
     def own_across(p):
         send(own_piece(p), at(mine, p), tok_ss.at[0, p], tok_rs.at[ACROSS, p], to_across)
@@ -192,27 +199,26 @@
     w_quarters = (g, g_prev, g_far, g_next)
 
     def w_own(i):
-        src, dst = w_own_at(i, g * WC, WC), w_at(2, i, g * WC, WC)
+        src, dst = w_own_at(i, g), w_at(2, i, g)
         send(src, dst, w_ss.at[0, i], w_rs.at[0, i], to_partner)
 
     def w_own_far(i):
-        src, dst = w_own_at(i, g_far * WC, WC), w_at(2, i, g_far * WC, WC)
+        src, dst = w_own_at(i, g_far), w_at(2, i, g_far)
         send(src, dst, w_ss.at[3, i], w_rs.at[2, i], to_partner)
 
     def w_sibling(i):
-        src, dst = w_own_at(i, 0, KC), w_at(1, i, 0, KC)
+        src, dst = w_own_at(i), w_at(1, i)
         send(src, dst, ws_ss.at[i], ws_rs.at[i], to_sibling)
 
     def w_arrived(cls, i):
-        arrived(("w", cls, i), w_at(2, i, w_quarters[cls] * WC, WC), w_rs.at[cls, i])
+        arrived(("w", cls, i), w_at(2, i, w_quarters[cls]), w_rs.at[cls, i])
 
     def w_forward(i, cls):
-        start = w_quarters[cls] * WC
-        src, dst = w_at(2, i, start, WC), w_at(3, i, start, WC)
+        src, dst = w_at(2, i, w_quarters[cls]), w_at(3, i, w_quarters[cls])
         send(src, dst, wf_ss.at[cls, i], wf_rs.at[cls, i], to_sibling)
 
     def w_send(i, q, n, cls, dev):
-        ref = w_at(2, i, q * WC, WC)
+        ref = w_at(2, i, q)
         send(ref, ref, w_ss.at[n, i], w_rs.at[cls, i], dev)
 
     def w_pass(i):
@@ -239,9 +245,9 @@
 
     def w_ready(i):
         once(("own w", i), w_copies[i])
-        arrived(("sibling w", i), w_at(1, i, 0, KC), ws_rs.at[i])
+        arrived(("sibling w", i), w_at(1, i), ws_rs.at[i])
         for cls, q in enumerate(w_quarters):
-            arrived(("other w", cls, i), w_at(3, i, q * WC, WC), wf_rs.at[cls, i])
+            arrived(("other w", cls, i), w_at(3, i, q), wf_rs.at[cls, i])
 
     def picked_places():
         picked = []
@@ -268,9 +274,15 @@
         rows = pl.ds(g * CAP, CAP)
         pltpu.make_async_copy(picks.at[rows], gets.at[rows], ad_ss.at[n, 0]).start()
 
+    picked = []
+
     def down_pick():
+        picked.extend(picked_places())
         down_copy.wait()
         adapters_send(0, dloc, dsend, drecv)
+        tok_copy.start()
+        for copy in w_copies:
+            copy.start()
 
     def up_pick():
         up_copy.wait()
@@ -300,7 +312,10 @@
         send(ref.at[0], ref.at[2], cp_ss.at[n, 0], cp_rs.at[n, 2], to_partner)
         send(ref.at[0], ref.at[1], cp_ss.at[n, 1], cp_rs.at[n, 1], to_sibling)
 
+    places = []
+
     def down_compact():
+        places.extend(request_places())
         adapters_arrived(0, drecv, dsend)
         for j in range(REQUESTS):
             dtmp[2 * j : 2 * j + 2, :] = drecv[places[j]].astype(F32)
@@ -337,20 +352,20 @@
             ref[...] = term
 
     def token_block(r, k):
-        rows = tok[:, START[r] : START[r] + PART[r], k * KC : (k + 1) * KC]
-        return rows.reshape(SOURCES * PART[r], KC)
+        rows = tok[:, START[r] : START[r] + PART[r], KSTART[k] : KSTART[k] + KCS[k]]
+        return rows.reshape(SOURCES * PART[r], KCS[k])
 
     def base(r, k, h):
         tok_ready(r, k)
         w_ready(h * NK + k)
-        weight = wbuf[h, k * KC : (k + 1) * KC, :]
+        weight = wbuf[h, KSTART[k] : KSTART[k] + KCS[k], :]
         term = jnp.dot(token_block(r, k), weight, preferred_element_type=F32)
         add(("base", r, h), acc[r].at[h], term)
 
     def low_rank(r, k):
         tok_ready(r, k)
         adapters_ready(0, dc)
-        rows = dc[:, :, k * KC : (k + 1) * KC].reshape(4 * 2 * REQUESTS, KC)
+        rows = dc[:, :, KSTART[k] : KSTART[k] + KCS[k]].reshape(8 * REQUESTS, KCS[k])
         term = lax.dot_general(
             rows, token_block(r, k), (((1,), (1,)), ((), ())), preferred_element_type=F32
         )
@@ -375,7 +390,11 @@
     z_low = jnp.minimum(z, z_partner)
     quad = z_low * 4 + x
 
+    first_late = []
+
     def codes_send(r):
+        if r == PARTS - 1:
+            first_late.append(len(sends))
         shape = (8 * REQUESTS, SOURCES * PART[r])
         row = lax.broadcasted_iota(jnp.int32, shape, 0)
         request = request_of(lax.broadcasted_iota(jnp.int32, shape, 1), r)
@@ -402,6 +421,11 @@
         return pltpu.make_async_copy(ost[r].at[h, 0], out_piece(z, c, r, h), sem)
 
     def codes_spread(r):
+        if r == PARTS - 1:
+            late = sends[first_late[0] :]
+            del sends[first_late[0] :]
+            sent()
+            sends.extend(late)
         z_other_low = 1 - z_low
         quad_low, quad_other = z_low * 4, z_other_low * 4
         for cls, q in (
@@ -453,43 +477,39 @@
         for m, (zz, cc) in enumerate(((z, 1 - c), (z_partner, c), (z_partner, 1 - c)), 1):
             arrived(("out", r, h, m), out_piece(zz, cc, r, h), out_rs.at[r, h, m])
 
-    picked = picked_places()
-    places = request_places()
-
     order = [
-        (w_own, 4), (w_sibling, 4), (w_own, 6), (own_across, 0), (own_sides, 0), (w_sibling, 0),
-        (w_sibling, 1), (w_own_far, 6), (w_own, 0), (w_own_far, 7), (w_sibling, 3), (w_sibling, 7),
-        (w_sibling, 2), (w_own, 7), (own_across, 1), (w_own, 5), (w_own, 3), (w_own, 2),
-        (own_sides, 1), (own_sides, 2), (own_across, 2), (w_sibling, 6), (w_own, 1), (w_sibling, 5),
-        (down_pick,), (own_sides, 3), (own_across, 3), (pass_left, 0), (w_pass, 4), (up_pick,),
-        (pass_across, 0), (w_pass_far, 6), (own_across, 4), (pass_left, 1), (pass_right, 1),
-        (pass_across, 2), (pass_right, 2), (down_compact,), (w_pass_far, 7), (w_pass, 0),
-        (w_pass_prev, 4), (w_pass_next, 4), (pass_left, 3), (pass_right, 3), (pass_across, 4),
-        (w_pass, 5), (w_pass, 7), (up_compact,), (pass_across_right, 2), (pass_across_left, 0),
-        (own_across, 5), (w_pass, 2), (w_pass_prev, 0), (w_pass_next, 0), (own_across, 6),
-        (own_across, 7), (pass_far, 1), (w_pass_far, 4), (w_pass_next, 5), (own_sides, 4),
-        (own_sides, 5), (w_pass, 6), (w_pass_prev, 5), (w_pass_next, 7), (own_sides, 6),
-        (pass_far, 3), (own_sides, 7), (pass_across_left, 4), (w_pass, 1), (w_pass_prev, 7),
-        (w_pass_next, 2), (pass_across, 6), (w_pass, 3), (w_pass_far, 5), (down_forward,),
-        (w_pass_prev, 2), (base, 0, 0, 1), (pass_left, 4), (w_pass_far, 0), (low_rank, 0, 2),
-        (w_pass_next, 6), (pass_left, 5), (pass_right, 5), (low_rank, 0, 0), (base, 0, 0, 0),
-        (base, 0, 1, 1), (w_pass_prev, 6), (pass_right, 6), (w_pass_next, 1), (pass_left, 7),
-        (pass_right, 7), (low_rank, 0, 1), (base, 0, 2, 1), (pass_across_right, 6),
-        (w_pass_prev, 1), (w_pass_next, 3), (low_rank, 0, 3), (base, 0, 3, 1), (codes_send, 0),
-        (base, 1, 0, 1), (pass_far, 7), (low_rank, 1, 0), (up_forward,), (base, 1, 0, 0),
-        (pass_far, 5), (base, 1, 2, 1), (low_rank, 1, 2), (w_pass_prev, 3), (codes_spread, 0),
-        (w_pass_far, 1), (finish, 0, 1), (w_pass_far, 2), (w_pass_far, 3), (base, 0, 1, 0),
-        (base, 1, 3, 1), (low_rank, 1, 3), (base, 0, 2, 0), (base, 0, 3, 0), (finish, 0, 0),
-        (low_rank, 1, 1), (codes_send, 1), (base, 1, 1, 0), (base, 1, 1, 1), (base, 1, 3, 0),
-        (base, 1, 2, 0), (codes_spread, 1), (finish, 1, 1), (finish, 1, 0),
+        (w_own, 2), (own_sides, 0), (w_own, 1), (w_sibling, 4), (w_own_far, 7), (w_own, 6),
+        (w_own, 5), (w_sibling, 1), (w_own, 0), (own_across, 0), (own_across, 1), (w_sibling, 2),
+        (w_sibling, 0), (w_sibling, 3), (w_sibling, 5), (w_own, 4), (own_sides, 1), (own_sides, 2),
+        (down_pick,), (up_pick,), (w_sibling, 7), (own_across, 2), (w_sibling, 6), (w_own_far, 6),
+        (w_own, 7), (own_sides, 3), (pass_left, 0), (w_own, 3), (own_across, 3), (pass_across, 0),
+        (w_pass_far, 7), (pass_left, 1), (pass_right, 1), (w_pass, 6), (down_compact,),
+        (pass_right, 2), (pass_across, 2), (w_pass, 5), (pass_left, 3), (pass_right, 3),
+        (w_pass, 0), (up_compact,), (w_pass, 4), (w_pass_far, 6), (w_pass_prev, 6),
+        (w_pass_next, 6), (w_pass, 2), (own_across, 4), (own_across, 5), (w_pass_prev, 5),
+        (w_pass_next, 5), (pass_across_left, 0), (w_pass, 7), (own_across, 6), (own_across, 7),
+        (w_pass, 3), (w_pass_prev, 0), (w_pass_next, 0), (pass_far, 1), (own_sides, 4),
+        (pass_across_right, 2), (w_pass_prev, 4), (w_pass_next, 4), (own_sides, 5), (own_sides, 6),
+        (pass_across, 4), (pass_far, 3), (w_pass_prev, 2), (w_pass_next, 2), (own_sides, 7),
+        (pass_across, 6), (w_pass_prev, 7), (w_pass_far, 5), (down_forward,), (w_pass_prev, 3),
+        (w_pass_next, 7), (w_pass, 1), (low_rank, 0, 0), (base, 0, 2, 1), (base, 0, 1, 1),
+        (pass_right, 5), (low_rank, 0, 2), (pass_left, 5), (w_pass_far, 0), (w_pass_next, 3),
+        (low_rank, 0, 1), (pass_right, 6), (pass_left, 4), (w_pass_next, 1), (base, 0, 0, 0),
+        (low_rank, 0, 3), (pass_across_left, 4), (w_pass_far, 4), (codes_send, 0), (pass_left, 7),
+        (pass_right, 7), (base, 0, 3, 1), (w_pass_far, 3), (base, 0, 0, 1), (pass_across_right, 6),
+        (w_pass_far, 2), (up_forward,), (pass_far, 5), (base, 0, 3, 0), (w_pass_far, 1),
+        (codes_spread, 0), (base, 0, 2, 0), (pass_far, 7), (w_pass_prev, 1), (finish, 0, 1),
+        (base, 1, 1, 1), (low_rank, 1, 2), (base, 1, 0, 0), (low_rank, 1, 1), (base, 1, 1, 0),
+        (base, 0, 1, 0), (low_rank, 1, 0), (base, 1, 3, 0), (low_rank, 1, 3), (codes_send, 1),
+        (finish, 0, 0), (base, 1, 3, 1), (base, 1, 0, 1), (base, 1, 2, 1), (base, 1, 2, 0),
+        (codes_spread, 1), (finish, 1, 0), (finish, 1, 1),
     ]
     for action, *args in order:
         action(*args)
     for r in range(PARTS):
         for h in range(HALVES):
             out_arrived(r, h)
-    for copy in sends:
-        copy.wait_send()
+    sent()
 
 
 def local(tokens, weight, down, up, lengths, request_adapter_id, adapter_storage_slot):

time: 87.7 us -> 85.3 us (0.973)
  Pallas kernels: 85.3 us -> 82.9 us
    pallas_call x1, Pallas kernels: 85.3 us -> 82.9 us  [local(): pl.pallas_call(kernel, out_shape=jax.ShapeDtypeStruct((2, SOURCES, 2, SHA...]
where the time goes in v3:
time: 85.3 us; the launch traced here: 85.2 us
  Pallas kernels  82.9 us (97%)
  local copies, waits for them, and re-layouts  2.26 us (3%)
    pallas_call x1, Pallas kernels, local(): pl.pallas_call(kernel, out_shape=jax.ShapeDtypeStruct((2, SOURCES, 2, SHA...  82.9 us
    unnamed x1, local copies, waits for them, and re-layouts  2.26 us

profile of v3, /device:TPU:1, one launch (start us, length us, event | category | flops | bytes accessed | tf_op | source)
XLA Modules:
  0.0 85.2 jit_solution(7179452666504611563)
XLA Ops:
  0.0 82.9 %shard_map.73 = bf16[2,8,2,64,256]{4,3,2,1,0:T(8,128)(2,1)} custom-call(bf16[64,8192]{1,0:T(8,128)(2,1)} %tok_hbm.1, bf16[8192,256]{1,0:T(8,128)(2,1)} %w_hbm.1, bf16[128,2,8192]{2,1,0:T(2,128)(2,1)} %down_hbm.1, bf16[128,64,256]{2,1,0:T(8,128)(2,1)} %up_hbm.1, s32[4,16]{1,0:T(4,128)} %len_ref.1, s32[4,16]{1,0:T(4,128)} %rid_ref.1, s32[512]{0:T(512)} %slot_ref.1), custom_call_target="tpu_custom_call" | custom-call | tf_op jit(solution)/shard_map/pallas_call | solution.py:520
  82.9 2.3 %copy.9 = bf16[2048,256]{1,0:T(8,128)(2,1)} copy(bf16[2048,256]{1,0:T(8,128)(2,1)} %bitcast.1) | data formatting | bytes 2097152

commit v4 on v3

--- a/solution.py
+++ b/solution.py
@@ -22,7 +22,7 @@
 LANES = 128
 HALVES = COLS // LANES
 SOURCES = 8
-KCS = (2304, 1792, 2304, 1792)
+KCS = (2176, 1920, 2176, 1920)
 NK = len(KCS)
 KSTART = tuple(sum(KCS[:k]) for k in range(NK))
 PIECES = PARTS * NK
@@ -450,27 +450,26 @@
             block = jnp.where(request == 2 * b, codes, 0.0).astype(BF16)
             spread[r][:, b * 128 : (b + 1) * 128] = block
 
-    def finish(r, h):
+    def finish(r, h, pair):
         adapters_ready(1, uc)
         lanes = slice(h * LANES, (h + 1) * LANES)
-        for pair in (1, 0):
-            table = jnp.concatenate(
-                [uc[m, :, :, lanes].reshape(REQUESTS * RANK, LANES) for m in (2 * pair, 2 * pair + 1)],
-                axis=1,
-            )
-            update = jnp.dot(spread[r][...], table, preferred_element_type=F32)
-            base_sum = acc[r][h, :, pair * 2 * LANES : (pair + 1) * 2 * LANES]
-            result = (base_sum + 0.5 * update).astype(BF16)
-            for n in (0, 1):
-                m = 2 * pair + n
-                piece = result[:, n * LANES : (n + 1) * LANES]
-                ost[r][h, m] = piece.reshape(SOURCES, PART[r], LANES)
-                if m == 0:
-                    out_local(r, h).start()
-                else:
-                    dev = (None, to_sibling, to_partner, to_partner_other)[m]
-                    ss, rs = out_ss.at[r, h, m], out_rs.at[r, h, m]
-                    send(ost[r].at[h, m], out_piece(z, c, r, h), ss, rs, dev)
+        table = jnp.concatenate(
+            [uc[m, :, :, lanes].reshape(REQUESTS * RANK, LANES) for m in (2 * pair, 2 * pair + 1)],
+            axis=1,
+        )
+        update = jnp.dot(spread[r][...], table, preferred_element_type=F32)
+        base_sum = acc[r][h, :, pair * 2 * LANES : (pair + 1) * 2 * LANES]
+        result = (base_sum + 0.5 * update).astype(BF16)
+        for n in (1, 0):
+            m = 2 * pair + n
+            piece = result[:, n * LANES : (n + 1) * LANES]
+            ost[r][h, m] = piece.reshape(SOURCES, PART[r], LANES)
+            if m == 0:
+                out_local(r, h).start()
+            else:
+                dev = (None, to_sibling, to_partner, to_partner_other)[m]
+                ss, rs = out_ss.at[r, h, m], out_rs.at[r, h, m]
+                send(ost[r].at[h, m], out_piece(z, c, r, h), ss, rs, dev)
 
     def out_arrived(r, h):
         out_local(r, h).wait()
@@ -478,31 +477,32 @@
             arrived(("out", r, h, m), out_piece(zz, cc, r, h), out_rs.at[r, h, m])
 
     order = [
-        (w_own, 2), (own_sides, 0), (w_own, 1), (w_sibling, 4), (w_own_far, 7), (w_own, 6),
-        (w_own, 5), (w_sibling, 1), (w_own, 0), (own_across, 0), (own_across, 1), (w_sibling, 2),
-        (w_sibling, 0), (w_sibling, 3), (w_sibling, 5), (w_own, 4), (own_sides, 1), (own_sides, 2),
-        (down_pick,), (up_pick,), (w_sibling, 7), (own_across, 2), (w_sibling, 6), (w_own_far, 6),
-        (w_own, 7), (own_sides, 3), (pass_left, 0), (w_own, 3), (own_across, 3), (pass_across, 0),
-        (w_pass_far, 7), (pass_left, 1), (pass_right, 1), (w_pass, 6), (down_compact,),
-        (pass_right, 2), (pass_across, 2), (w_pass, 5), (pass_left, 3), (pass_right, 3),
-        (w_pass, 0), (up_compact,), (w_pass, 4), (w_pass_far, 6), (w_pass_prev, 6),
-        (w_pass_next, 6), (w_pass, 2), (own_across, 4), (own_across, 5), (w_pass_prev, 5),
-        (w_pass_next, 5), (pass_across_left, 0), (w_pass, 7), (own_across, 6), (own_across, 7),
-        (w_pass, 3), (w_pass_prev, 0), (w_pass_next, 0), (pass_far, 1), (own_sides, 4),
-        (pass_across_right, 2), (w_pass_prev, 4), (w_pass_next, 4), (own_sides, 5), (own_sides, 6),
-        (pass_across, 4), (pass_far, 3), (w_pass_prev, 2), (w_pass_next, 2), (own_sides, 7),
-        (pass_across, 6), (w_pass_prev, 7), (w_pass_far, 5), (down_forward,), (w_pass_prev, 3),
-        (w_pass_next, 7), (w_pass, 1), (low_rank, 0, 0), (base, 0, 2, 1), (base, 0, 1, 1),
-        (pass_right, 5), (low_rank, 0, 2), (pass_left, 5), (w_pass_far, 0), (w_pass_next, 3),
-        (low_rank, 0, 1), (pass_right, 6), (pass_left, 4), (w_pass_next, 1), (base, 0, 0, 0),
-        (low_rank, 0, 3), (pass_across_left, 4), (w_pass_far, 4), (codes_send, 0), (pass_left, 7),
-        (pass_right, 7), (base, 0, 3, 1), (w_pass_far, 3), (base, 0, 0, 1), (pass_across_right, 6),
-        (w_pass_far, 2), (up_forward,), (pass_far, 5), (base, 0, 3, 0), (w_pass_far, 1),
-        (codes_spread, 0), (base, 0, 2, 0), (pass_far, 7), (w_pass_prev, 1), (finish, 0, 1),
-        (base, 1, 1, 1), (low_rank, 1, 2), (base, 1, 0, 0), (low_rank, 1, 1), (base, 1, 1, 0),
-        (base, 0, 1, 0), (low_rank, 1, 0), (base, 1, 3, 0), (low_rank, 1, 3), (codes_send, 1),
-        (finish, 0, 0), (base, 1, 3, 1), (base, 1, 0, 1), (base, 1, 2, 1), (base, 1, 2, 0),
-        (codes_spread, 1), (finish, 1, 0), (finish, 1, 1),
+        (own_sides, 0), (w_own, 1), (own_across, 0), (w_sibling, 1), (w_own_far, 6), (w_sibling, 6),
+        (w_sibling, 3), (own_across, 1), (own_across, 2), (w_own, 3), (w_own, 4), (w_sibling, 5),
+        (w_own, 0), (w_own, 2), (w_sibling, 4), (w_sibling, 2), (own_sides, 1), (own_sides, 2),
+        (down_pick,), (w_pass, 1), (up_pick,), (own_across, 3), (own_sides, 3), (pass_across, 0),
+        (w_sibling, 0), (w_own_far, 7), (w_sibling, 7), (pass_left, 0), (w_own, 7), (w_pass_far, 6),
+        (w_own, 5), (w_own, 6), (own_across, 4), (pass_left, 1), (pass_right, 1), (down_compact,),
+        (w_pass, 0), (pass_right, 2), (w_pass_prev, 1), (pass_across, 2), (w_pass_next, 1),
+        (w_pass, 4), (pass_left, 3), (pass_right, 3), (pass_across, 4), (w_pass, 2),
+        (w_pass_far, 7), (pass_across_left, 0), (w_pass, 7), (up_compact,), (own_across, 5),
+        (w_pass, 3), (own_across, 6), (w_pass_next, 0), (w_pass_prev, 0), (own_across, 7),
+        (w_pass_far, 1), (w_pass_prev, 4), (pass_far, 1), (pass_across_right, 2), (own_sides, 4),
+        (w_pass_next, 4), (w_pass_prev, 2), (own_sides, 5), (own_sides, 6), (pass_far, 3),
+        (w_pass_prev, 7), (w_pass_next, 2), (own_sides, 7), (pass_across_left, 4), (w_pass, 6),
+        (w_pass_prev, 3), (w_pass_next, 7), (pass_across, 6), (down_forward,), (w_pass, 5),
+        (w_pass_next, 3), (w_pass_far, 0), (low_rank, 0, 0), (pass_left, 4), (low_rank, 0, 2),
+        (base, 0, 0, 0), (base, 0, 1, 0), (w_pass_far, 4), (w_pass_next, 6), (pass_left, 5),
+        (pass_right, 5), (low_rank, 0, 1), (pass_right, 6), (base, 0, 0, 1), (w_pass_next, 5),
+        (pass_left, 7), (pass_right, 7), (w_pass_far, 2), (low_rank, 0, 3), (codes_send, 0),
+        (base, 0, 3, 1), (pass_across_right, 6), (base, 0, 2, 0), (w_pass_far, 3), (w_pass_prev, 6),
+        (up_forward,), (pass_far, 7), (low_rank, 1, 0), (base, 0, 3, 0), (base, 1, 0, 0),
+        (base, 1, 0, 1), (codes_spread, 0), (pass_far, 5), (base, 1, 2, 1), (finish, 0, 0, 1),
+        (w_pass_prev, 5), (base, 1, 3, 0), (low_rank, 1, 2), (base, 1, 2, 0), (w_pass_far, 5),
+        (low_rank, 1, 3), (base, 1, 3, 1), (base, 0, 2, 1), (low_rank, 1, 1), (codes_send, 1),
+        (base, 0, 1, 1), (finish, 0, 1, 1), (base, 1, 1, 1), (base, 1, 1, 0), (finish, 0, 0, 0),
+        (finish, 0, 1, 0), (codes_spread, 1), (finish, 1, 1, 1), (finish, 1, 0, 1),
+        (finish, 1, 1, 0), (finish, 1, 0, 0),
     ]
     for action, *args in order:
         action(*args)

time: 85.3 us -> 84.7 us (level)
  no operation moved by 1% of the time
where the time goes in v4:
time: 84.7 us; the launch traced here: 84.5 us
  Pallas kernels  82.2 us (97%)
  local copies, waits for them, and re-layouts  2.26 us (3%)
    pallas_call x1, Pallas kernels, local(): pl.pallas_call(kernel, out_shape=jax.ShapeDtypeStruct((2, SOURCES, 2, SHA...  82.2 us
    unnamed x1, local copies, waits for them, and re-layouts  2.26 us

profile of v4, /device:TPU:1, one launch (start us, length us, event | category | flops | bytes accessed | tf_op | source)
XLA Modules:
  0.0 84.5 jit_solution(4936834433233273876)
XLA Ops:
  0.0 82.2 %shard_map.73 = bf16[2,8,2,64,256]{4,3,2,1,0:T(8,128)(2,1)} custom-call(bf16[64,8192]{1,0:T(8,128)(2,1)} %tok_hbm.1, bf16[8192,256]{1,0:T(8,128)(2,1)} %w_hbm.1, bf16[128,2,8192]{2,1,0:T(2,128)(2,1)} %down_hbm.1, bf16[128,64,256]{2,1,0:T(8,128)(2,1)} %up_hbm.1, s32[4,16]{1,0:T(4,128)} %len_ref.1, s32[4,16]{1,0:T(4,128)} %rid_ref.1, s32[512]{0:T(512)} %slot_ref.1), custom_call_target="tpu_custom_call" | custom-call | tf_op jit(solution)/shard_map/pallas_call | solution.py:520
  82.3 2.3 %copy.9 = bf16[2048,256]{1,0:T(8,128)(2,1)} copy(bf16[2048,256]{1,0:T(8,128)(2,1)} %bitcast.1) | data formatting | bytes 2097152

commit v5 on v4

--- a/solution.py
+++ b/solution.py
@@ -37,11 +37,13 @@
     tok_hbm, w_hbm, down_hbm, up_hbm, len_ref, rid_ref, slot_ref, out_hbm,
     tok, wbuf, dloc, uloc, dsend, usend, drecv, urecv, dtmp, dc, uc,
     acc0, acc1, part0, part1, shr0, shr1, spread0, spread1, ost0, ost1,
+    rows0, rows1, lanes0, lanes1,
     loc_sem, own_sem, tok_ss, tok_rs, w_ss, w_rs, ws_ss, ws_rs, wf_ss, wf_rs,
     ad_ss, ad_rs, cp_ss, cp_rs, sh_ss, sh_rs, out_ss, out_rs,
 ):
     acc, part, shr = (acc0, acc1), (part0, part1), (shr0, shr1)
     spread, ost = (spread0, spread1), (ost0, ost1)
+    by_lane, by_row = (rows0, rows1), (lanes0, lanes1)
     g = lax.axis_index("group")
     tp = lax.axis_index("tp")
     z = tp // 8
@@ -392,12 +394,18 @@
 
     first_late = []
 
+    def requests_find(r):
+        shape = (8 * REQUESTS, SOURCES * PART[r])
+        by_lane[r][...] = request_of(lax.broadcasted_iota(jnp.int32, shape, 1), r)
+        shape = (SOURCES * PART[r], 128)
+        by_row[r][...] = request_of(lax.broadcasted_iota(jnp.int32, shape, 0), r)
+
     def codes_send(r):
         if r == PARTS - 1:
             first_late.append(len(sends))
         shape = (8 * REQUESTS, SOURCES * PART[r])
         row = lax.broadcasted_iota(jnp.int32, shape, 0)
-        request = request_of(lax.broadcasted_iota(jnp.int32, shape, 1), r)
+        request = by_lane[r][...]
         masked = jnp.where(request == (row % 32) // 2, part[r][...], 0.0).astype(BF16)
         lane = lax.broadcasted_iota(jnp.int32, (16, 128), 1)
         member = lane // 32
@@ -443,7 +451,7 @@
         hrows = SOURCES * PART[r]
         codes = shr[r][...].reshape(RANK, hrows).astype(BF16)
         codes = lax.dot_general(codes, order, (((0,), (0,)), ((), ())), preferred_element_type=F32)
-        request = request_of(lax.broadcasted_iota(jnp.int32, (hrows, 128), 0), r)
+        request = by_row[r][...]
         half = lax.broadcasted_iota(jnp.int32, (hrows, 128), 1) // RANK
         request = request - half
         for b in range(REQUESTS // 2):
@@ -480,7 +488,7 @@
         (own_sides, 0), (w_own, 1), (own_across, 0), (w_sibling, 1), (w_own_far, 6), (w_sibling, 6),
         (w_sibling, 3), (own_across, 1), (own_across, 2), (w_own, 3), (w_own, 4), (w_sibling, 5),
         (w_own, 0), (w_own, 2), (w_sibling, 4), (w_sibling, 2), (own_sides, 1), (own_sides, 2),
-        (down_pick,), (w_pass, 1), (up_pick,), (own_across, 3), (own_sides, 3), (pass_across, 0),
+        (down_pick,), (w_pass, 1), (up_pick,), (requests_find, 0), (requests_find, 1), (own_across, 3), (own_sides, 3), (pass_across, 0),
         (w_sibling, 0), (w_own_far, 7), (w_sibling, 7), (pass_left, 0), (w_own, 7), (w_pass_far, 6),
         (w_own, 5), (w_own, 6), (own_across, 4), (pass_left, 1), (pass_right, 1), (down_compact,),
         (w_pass, 0), (pass_right, 2), (w_pass_prev, 1), (pass_across, 2), (w_pass_next, 1),
@@ -539,6 +547,8 @@
             *(pltpu.VMEM((SOURCES, 8, SOURCES * n), F32) for n in PART),
             *(pltpu.VMEM((SOURCES * n, REQUESTS * RANK), BF16) for n in PART),
             *(pltpu.VMEM((HALVES, 4, SOURCES, n, LANES), BF16) for n in PART),
+            *(pltpu.VMEM((8 * REQUESTS, SOURCES * n), jnp.int32) for n in PART),
+            *(pltpu.VMEM((SOURCES * n, 128), jnp.int32) for n in PART),
             dma((3 + PARTS * HALVES,)),
             dma((CHUNKS,)),
             dma((7, PIECES)),

time: 84.7 us -> 84.4 us (level)
  no operation moved by 1% of the time
where the time goes in v5:
time: 84.4 us; the launch traced here: 84.2 us
  Pallas kernels  82 us (97%)
  local copies, waits for them, and re-layouts  2.26 us (3%)
    pallas_call x1, Pallas kernels, local(): pl.pallas_call(kernel, out_shape=jax.ShapeDtypeStruct((2, SOURCES, 2, SHA...  82 us
    unnamed x1, local copies, waits for them, and re-layouts  2.26 us

profile of v5, /device:TPU:1, one launch (start us, length us, event | category | flops | bytes accessed | tf_op | source)
XLA Modules:
  0.0 84.2 jit_solution(4820202260384050312)
XLA Ops:
  0.0 82.0 %shard_map.73 = bf16[2,8,2,64,256]{4,3,2,1,0:T(8,128)(2,1)} custom-call(bf16[64,8192]{1,0:T(8,128)(2,1)} %tok_hbm.1, bf16[8192,256]{1,0:T(8,128)(2,1)} %w_hbm.1, bf16[128,2,8192]{2,1,0:T(2,128)(2,1)} %down_hbm.1, bf16[128,64,256]{2,1,0:T(8,128)(2,1)} %up_hbm.1, s32[4,16]{1,0:T(4,128)} %len_ref.1, s32[4,16]{1,0:T(4,128)} %rid_ref.1, s32[512]{0:T(512)} %slot_ref.1), custom_call_target="tpu_custom_call" | custom-call | tf_op jit(solution)/shard_map/pallas_call | solution.py:528
  82.0 2.3 %copy.9 = bf16[2048,256]{1,0:T(8,128)(2,1)} copy(bf16[2048,256]{1,0:T(8,128)(2,1)} %bitcast.1) | data formatting | bytes 2097152
